TPU v7x, 128 devices: a whole 4x4x4 slice. The times are simulated.
128 devices in a mesh: kvp: 16 (over y, x), head: 8 (over z, core).
Axes of the slice: x: 4, y: 4, z: 4, core: 2. Of those that a mesh axis runs over, the one named last changes fastest.
Arguments:
- hidden_in: bfloat16 [64, 8192], P(None, 'kvp'), may hold values from -32 to 32
- norm_gain: bfloat16 [8192], P('kvp'), may hold values from 0.25 to 1.75
- w_query: bfloat16 [8192, 8192], P('kvp', 'head'), may hold values from -0.0625 to 0.0625
- w_key: bfloat16 [8192, 1024], P('kvp', 'head'), may hold values from -0.375 to 0.375
- w_value: bfloat16 [8192, 1024], P('kvp', 'head'), may hold values from -0.0625 to 0.0625
- w_out: bfloat16 [8192, 8192], P('head', 'kvp'), may hold values from -0.0625 to 0.0625
- post_gain: bfloat16 [8192], P('kvp'), may hold values from 0.25 to 1.75
- w_gate: bfloat16 [8192, 28672], P('kvp', 'head'), may hold values from -0.0625 to 0.0625
- w_up: bfloat16 [8192, 28672], P('kvp', 'head'), may hold values from -0.0625 to 0.0625
- w_down: bfloat16 [28672, 8192], P('head', 'kvp'), may hold values from -0.03125 to 0.03125
- cache_keys: bfloat16 [2560, 128, 1024], P('kvp', None, 'head'), may hold values from -128 to 128
- cache_values: bfloat16 [2560, 128, 1024], P('kvp', None, 'head'), may hold values from -6 to 6
- context_len: int32 [16], replicated, may hold values from 3969 to 28672, as said below
- slot_request: int32 [2560], P('kvp'), may hold values from -1 to 15, as said below
- slot_start: int32 [2560], P('kvp'), may hold values from 0 to 28544, as said below
Outputs:
- next_hidden: bfloat16 [64, 8192], P(None, 'kvp')
- draft_keys: bfloat16 [64, 1024], P(None, 'head')
- draft_values: bfloat16 [64, 1024], P(None, 'head')
Inputs may be any that keep to these rules, and one draw needn't show every extreme that they name: Each request's cached tokens fill ceil(context_len / 128) blocks, between 32 and 224; the requests' blocks total 128 * 16. `slot_request`: every block of every request has exactly one slot. The 160 slots of a kvp device hold between 96 and 160 live blocks, which come first, and some device has all 160 live. A request's blocks stand in order in consecutive slots, continuing on the next kvp devices. `slot_start`: a multiple of 128; the slot holds tokens slot_start to slot_start + 127 of its request; 0 for empty slots.
All inputs are finite; a program needn't handle non-finite values.
Results may differ from a plain program's by a relative error of at most 0.017.
Values may be sent and summed in bfloat16 or wider, within the bound.
A program may use at most 128 MiB of HBM per device.

v0:
```python
import math

import jax
import jax.numpy as jnp
from jax import lax
from jax.sharding import PartitionSpec as P

D = 8192
HD = 128
DRAFT = 4
BLOCK = 128


EPSILON = 1e-05
THETA_BASE = 500000.0
FLOOR_SCORE = -1e30


def joined(part, axis, combine):
    gathered = jax.tree.map(lambda a: lax.all_gather(a, axis), part)

    def take(source):
        return jax.tree.map(lambda a: lax.dynamic_index_in_dim(a, source, 0, False), gathered)

    return lax.fori_loop(
        1, lax.axis_size(axis), lambda source, state: combine(state, take(source)), take(0)
    )


def rotate(vectors, positions):
    half_dim = vectors.shape[-1] // 2
    exponent = jnp.arange(half_dim, dtype=jnp.float32) * (2.0 / vectors.shape[-1])
    frequency = THETA_BASE ** (-exponent)
    angles = positions.astype(jnp.float32)[..., None, None] * frequency
    cosine = jnp.cos(angles)
    sine_part = jnp.sin(angles)
    first_half = vectors[..., :half_dim]
    second_half = vectors[..., half_dim:]
    return jnp.concatenate(
        [
            first_half * cosine - second_half * sine_part,
            second_half * cosine + first_half * sine_part,
        ],
        axis=-1,
    )


def combine_parts(earlier, later):
    first_max, first_sum, first_out = earlier
    second_max, second_sum, second_out = later
    highest = jnp.maximum(first_max, second_max)
    first_scale = jnp.exp(first_max - highest)
    second_scale = jnp.exp(second_max - highest)
    return (
        highest,
        first_sum * first_scale + second_sum * second_scale,
        first_out * first_scale[..., None] + second_out * second_scale[..., None],
    )


def heads_to_rows(finished, kv_here, groups):
    item_count = finished.shape[0]
    return (
        finished.reshape(item_count, kv_here, DRAFT, groups, HD)
        .transpose(0, 2, 1, 3, 4)
        .reshape(item_count * DRAFT, kv_here * groups * HD)
    )


def body(
    hidden_in,
    norm_gain,
    w_query,
    w_key,
    w_value,
    w_out,
    post_gain,
    w_gate,
    w_up,
    w_down,
    cache_keys,
    cache_values,
    context_len,
    slot_request,
    slot_start,
):
    row_count = hidden_in.shape[0]
    kv_devices = lax.axis_size("kvp")
    kv_position = lax.axis_index("kvp")
    request_count = context_len.shape[0]
    heads_here = w_query.shape[1] // HD
    kv_here = w_key.shape[1] // HD
    groups = heads_here // kv_here
    query_rows = DRAFT * groups
    score_scale = 1.0 / math.sqrt(HD)
    hidden_f = hidden_in.astype(jnp.float32)
    scaled_in = (hidden_f * norm_gain.astype(jnp.float32)).astype(jnp.bfloat16)
    square_part = jnp.sum(hidden_f * hidden_f, axis=1, keepdims=True)
    query_part = jnp.dot(scaled_in, w_query, preferred_element_type=jnp.float32)
    key_part = jnp.dot(scaled_in, w_key, preferred_element_type=jnp.float32)
    value_part = jnp.dot(scaled_in, w_value, preferred_element_type=jnp.float32)
    square_sum, query_raw, key_raw, value_raw = lax.psum(
        (square_part, query_part, key_part, value_part), "kvp"
    )
    inverse = lax.rsqrt(square_sum / D + EPSILON)
    query_raw = inverse * query_raw
    key_raw = inverse * key_raw
    value_raw = inverse * value_raw
    positions = context_len[:, None] + jnp.arange(DRAFT, dtype=jnp.int32)[None, :]
    queries = rotate(query_raw.reshape(request_count, DRAFT, heads_here, HD), positions).astype(
        jnp.bfloat16
    )
    draft_keys = rotate(key_raw.reshape(request_count, DRAFT, kv_here, HD), positions).astype(
        jnp.bfloat16
    )
    draft_values = value_raw.astype(jnp.bfloat16)
    grouped = (
        queries.reshape(request_count, DRAFT, kv_here, groups, HD)
        .transpose(0, 2, 1, 3, 4)
        .reshape(request_count, kv_here, query_rows, HD)
    )
    new_keys = draft_keys.transpose(0, 2, 1, 3)
    new_values = draft_values.reshape(request_count, DRAFT, kv_here, HD).transpose(0, 2, 1, 3)
    draft_scores = (
        jnp.einsum("bkqd,bktd->bkqt", grouped, new_keys, preferred_element_type=jnp.float32)
        * score_scale
    )
    row_step = jnp.arange(query_rows, dtype=jnp.int32) // groups
    causal = (jnp.arange(DRAFT, dtype=jnp.int32)[None, :] <= row_step[:, None])[None, None, :, :]
    draft_max_all = jnp.max(jnp.where(causal, draft_scores, FLOOR_SCORE), axis=-1)
    draft_weights = jnp.where(causal, jnp.exp(draft_scores - draft_max_all[..., None]), 0.0)
    draft_sum_all = jnp.sum(draft_weights, axis=-1)
    draft_out_all = jnp.einsum(
        "bkqt,bktd->bkqd",
        draft_weights.astype(jnp.bfloat16),
        new_values,
        preferred_element_type=jnp.float32,
    )
    owner_mask = (jnp.arange(request_count, dtype=jnp.int32) % kv_devices == kv_position)[
        :, None, None
    ]
    draft_owned = (
        jnp.where(owner_mask, draft_max_all, FLOOR_SCORE),
        jnp.where(owner_mask, draft_sum_all, 0.0),
        jnp.where(owner_mask[..., None], draft_out_all, 0.0),
    )
    slot_total = slot_request.shape[0]
    safe_req = jnp.clip(slot_request, 0, request_count - 1)
    chosen = jnp.take(grouped, safe_req, axis=0)
    slot_keys = cache_keys.reshape(slot_total, BLOCK, kv_here, HD)
    slot_values = cache_values.reshape(slot_total, BLOCK, kv_here, HD)
    scores = (
        jnp.einsum("skqd,stkd->skqt", chosen, slot_keys, preferred_element_type=jnp.float32)
        * score_scale
    )
    token_pos = slot_start[:, None] + jnp.arange(BLOCK, dtype=jnp.int32)[None, :]
    limits = jnp.take(context_len, safe_req)
    live_mask = ((slot_request[:, None] >= 0) & (token_pos < limits[:, None]))[:, None, None, :]
    block_max = jnp.max(jnp.where(live_mask, scores, FLOOR_SCORE), axis=-1)
    weights = jnp.where(live_mask, jnp.exp(scores - block_max[..., None]), 0.0)
    block_sum = jnp.sum(weights, axis=-1)
    block_out = jnp.einsum(
        "skqt,stkd->skqd",
        weights.astype(jnp.bfloat16),
        slot_values,
        preferred_element_type=jnp.float32,
    )
    request_ids = jnp.arange(request_count, dtype=jnp.int32)
    member = (slot_request[:, None] == request_ids[None, :])[:, :, None, None]
    slot_max = jnp.max(jnp.where(member, block_max[:, None], FLOOR_SCORE), axis=0)
    factor = jnp.where(member, jnp.exp(block_max[:, None] - slot_max[None]), 0.0)
    slot_sum = jnp.sum(factor * block_sum[:, None], axis=0)
    slot_out = jnp.einsum("sbkq,skqd->bkqd", factor, block_out, precision=lax.Precision.HIGHEST)
    local_max, local_sum, local_out = combine_parts((slot_max, slot_sum, slot_out), draft_owned)
    whole_max, whole_sum, whole_out = joined(
        (local_max, local_sum, local_out), "kvp", combine_parts
    )
    attention = heads_to_rows(
        (whole_out / whole_sum[..., None]).astype(jnp.bfloat16), kv_here, groups
    )
    attn_part = jnp.dot(attention, w_out, preferred_element_type=jnp.float32)
    attn_full = lax.psum(attn_part.astype(jnp.bfloat16), "head").astype(jnp.float32)
    residual = (hidden_f + attn_full).astype(jnp.bfloat16)
    residual_f = residual.astype(jnp.float32)
    post_square = lax.psum(jnp.sum(residual_f * residual_f, axis=1, keepdims=True), "kvp")
    normed = (
        residual_f * post_gain.astype(jnp.float32) * lax.rsqrt(post_square / D + EPSILON)
    ).astype(jnp.bfloat16)
    gate_part = jnp.dot(normed, w_gate, preferred_element_type=jnp.float32)
    up_part = jnp.dot(normed, w_up, preferred_element_type=jnp.float32)
    gate_sum, up_sum = (
        lax.psum(gate_part.astype(jnp.bfloat16), "kvp").astype(jnp.float32),
        lax.psum(up_part.astype(jnp.bfloat16), "kvp").astype(jnp.float32),
    )
    hidden_mid = (jax.nn.silu(gate_sum) * up_sum).astype(jnp.bfloat16)
    down_part = jnp.dot(hidden_mid, w_down, preferred_element_type=jnp.float32)
    down_sum = lax.psum(down_part.astype(jnp.bfloat16), "head").astype(jnp.float32)
    next_hidden = (residual_f + down_sum).astype(jnp.bfloat16)
    return (next_hidden, draft_keys.reshape(row_count, kv_here * HD), draft_values)


def solution(mesh):
    return jax.shard_map(
        body,
        mesh=mesh,
        in_specs=(
            P(None, "kvp"),
            P("kvp"),
            P("kvp", "head"),
            P("kvp", "head"),
            P("kvp", "head"),
            P("head", "kvp"),
            P("kvp"),
            P("kvp", "head"),
            P("kvp", "head"),
            P("head", "kvp"),
            P("kvp", None, "head"),
            P("kvp", None, "head"),
            P(),
            P("kvp"),
            P("kvp"),
        ),
        out_specs=(P(None, "kvp"), P(None, "head"), P(None, "head")),
        check_vma=False,
    )
```

profile of v0, /device:TPU:1, one launch (start us, length us, event | category | flops | bytes accessed | tf_op | source)
XLA Modules:
  0.0 537.7 jit_solution(13371129736174976476)
XLA Ops:
  7.2 1.6 fusion.40
  9.5 1.7 fusion.53
  11.2 1.7 fusion.51
  13.0 1.8 fusion.55
  14.9 0.7 add_convert_fusion.1
  15.6 1.9 fusion.92
  17.6 0.7 broadcast_compare_fusion
  19.0 10.5 %fusion.82 = (s32[160]{0:T(256)S(1)}, s32[160]{0:T(256)S(1)}) fusion(s32[]{:T(128)} %bitcast.5, s32[]{:T(128)} %bitcast.6, s32[]{:T(128)} %bitcast.7, s32[]{:T(128)} %bitcast.8, s32[]{:T(128)} %bitcast.9, s32[]{:T(128)} %bitcast.10, s32[]{:T(128)} %bitcast.11, s32[]{:T(128)} %bitcast.12, s32[]{:T(128)} %bitcast.13, s32[]{:T(128)} %bitcast.14, s32[]{:T(128)} %bitcast.15, ...), kind=kLoop, calls=%fused_computation.139 | loop fusion | flops 6080 | bytes 1984 | tf_op jit(solution)/shard_map/jit(_take)/select_n | solution.py:157
  29.8 0.8 fusion.50
  30.7 65.5 %all-reduce.14.cloned.1.call-done = (f32[64,1]{0,1:T(1,128)}, f32[64,128]{1,0:T(8,128)}, f32[64,128]{1,0:T(8,128)}) async-done(((f32[64,1]{0,1:T(1,128)}, f32[64,128]{1,0:T(8,128)}, f32[64,128]{1,0:T(8,128)}), (f32[64,1]{0,1:T(1,128)}, f32[64,128]{1,0:T(8,128)}, f32[64,128]{1,0:T(8,128)})) %all-reduce.14.cloned.1.call-update) | async-done | bytes 65808 | tf_op jit(solution)/shard_map/psum | solution.py:102
  96.8 0.9 multiply_convert_fusion
  98.0 85.5 %all-reduce.8.cloned.1.call-done = f32[64,1024]{1,0:T(8,128)} async-done(((f32[64,1024]{1,0:T(8,128)}), f32[64,1024]{1,0:T(8,128)}) %all-reduce.8.cloned.1.call-update) | async-done | bytes 262160 | tf_op jit(solution)/shard_map/psum | solution.py:102
  183.5 1.0 multiply_bitcast_fusion
  184.9 0.8 gather_fusion
  185.7 6.9 %select_reduce_fusion = (f32[160,32]{1,0:T(8,128)S(1)}, f32[160,32,128]{2,1,0:T(8,128)}) fusion(pred[160,128]{1,0:T(8,128)(4,1)S(1)} %fusion.50, bf16[160,128,128]{2,1,0:T(8,128)(2,1)} %param.27, bf16[160,32,128]{2,1,0:T(8,128)(2,1)S(1)} %gather_fusion, pred[160]{0:T(512)(128)(4,1)S(1)} %get-tuple-element.248), kind=kOutput, calls=%fused_computation.15 | convolution fusion | flops 170388480 | bytes 9216160 | tf_op jit(solution)/shard_map/skqd,stkd->skqt/dot_general | solution.py:153
  193.5 4.8 fusion.6
  198.6 4.6 fusion.21
  203.2 2.9 fusion.5
  206.6 17.8 %all_gather.14 = f32[16,16,1,32]{3,1,2,0:T(8,128)S(1)} all-gather(f32[1,16,1,32]{3,1,2,0:T(8,128)S(1)} %get-tuple-element.244), channel_id=1, replica_groups=mesh['kvp'=16,'head'=8] {'kvp'}, dimensions={0}, use_global_device_ids=true | all-gather | bytes 34816 | tf_op jit(solution)/shard_map/all_gather | solution.py:20
  224.4 17.4 %all_gather.15 = f32[16,16,1,32]{3,1,2,0:T(8,128)S(1)} all-gather(f32[1,16,1,32]{3,1,2,0:T(8,128)S(1)} %get-tuple-element.243), channel_id=1, replica_groups=mesh['kvp'=16,'head'=8] {'kvp'}, dimensions={0}, use_global_device_ids=true | all-gather | bytes 34816 | tf_op jit(solution)/shard_map/all_gather | solution.py:20
  241.9 19.6 %all-gather.3.cloned.1.call-done = f32[256,1,32,128]{3,0,2,1:T(8,128)} async-done(((f32[16,1,32,128]{3,0,2,1:T(8,128)}), f32[256,1,32,128]{3,0,2,1:T(8,128)}) %all-gather.3.cloned.1.call-update) | async-done | bytes 4194320 | tf_op jit(solution)/shard_map/all_gather | solution.py:20
  261.4 1.0 slice.43
  262.5 20.0 %while.19 = (s32[]{:T(128)}, f32[16,1,32]{2,1,0:T(1,128)S(1)}, f32[16,1,32]{2,1,0:T(1,128)S(1)}, f32[16,1,32,128]{3,2,1,0:T(8,128)S(1)}, f32[16,16,1,32]{3,1,2,0...) while((s32[]{:T(128)}, f32[16,1,32]{2,1,0:T(1,128)S(1)}, ...), condition=%wide.region_12.13_spmd, body=%wide.region_11.12_spmd.sunk | while | flops 199685 | bytes 1339543 | solution.py:25
  262.6 1.1 constant_dynamic-slice_fusion.6
  264.0 1.0 constant_dynamic-slice_fusion.6
  265.3 1.0 constant_dynamic-slice_fusion.6
  266.7 1.0 constant_dynamic-slice_fusion.6
  268.0 1.0 constant_dynamic-slice_fusion.6
  269.3 1.0 constant_dynamic-slice_fusion.6
  270.6 1.0 constant_dynamic-slice_fusion.6
  272.0 1.0 constant_dynamic-slice_fusion.6
  273.3 1.0 constant_dynamic-slice_fusion.6
  274.6 1.0 constant_dynamic-slice_fusion.6
  276.0 1.0 constant_dynamic-slice_fusion.6
  277.3 1.0 constant_dynamic-slice_fusion.6
  278.6 1.0 constant_dynamic-slice_fusion.6
  279.9 1.0 constant_dynamic-slice_fusion.6
  281.3 1.0 constant_dynamic-slice_fusion.6
  282.8 0.9 convolution_convert_fusion.2
  283.8 57.0 %all-reduce.10.cloned.1.call-done = bf16[64,512]{1,0:T(8,128)(2,1)} async-done(((bf16[64,512]{1,0:T(8,128)(2,1)}), bf16[64,512]{1,0:T(8,128)(2,1)}) %all-reduce.10.cloned.1.call-update) | async-done | bytes 65552 | tf_op jit(solution)/shard_map/psum | solution.py:182
  340.8 1.0 fusion.45
  341.8 33.3 %psum.68 = f32[64,1]{0,1:T(1,128)S(1)} all-reduce(f32[64,1]{0,1:T(1,128)S(1)} %bitcast.164), channel_id=1, replica_groups=mesh['kvp'=16,'head'=8] {'kvp'}, use_global_device_ids=true, to_apply=%region_15.16 | all-reduce | flops 64 | bytes 512 | tf_op jit(solution)/shard_map/psum | solution.py:185
  375.1 3.8 convolution_convert_fusion
  378.9 1.6 convolution_convert_fusion.1
  380.5 87.4 %all-reduce.16.cloned.1.call-done = (bf16[64,3584]{1,0:T(8,128)(2,1)}, bf16[64,3584]{1,0:T(8,128)(2,1)}) async-done(((bf16[64,3584]{1,0:T(8,128)(2,1)}, bf16[64,3584]{1,0:T(8,128)(2,1)}), (bf16[64,3584]{1,0:T(8,128)(2,1)}, bf16[64,3584]{1,0:T(8,128)(2,1)})) %all-reduce.16.cloned.1.call-update) | async-done | bytes 917520 | tf_op jit(solution)/shard_map/psum | solution.py:193
  468.0 3.7 convolution_convert_fusion.3
  472.4 57.0 %all-reduce.12.cloned.1.call-done = bf16[64,512]{1,0:T(8,128)(2,1)} async-done(((bf16[64,512]{1,0:T(8,128)(2,1)}), bf16[64,512]{1,0:T(8,128)(2,1)}) %all-reduce.12.cloned.1.call-update) | async-done | bytes 65552 | tf_op jit(solution)/shard_map/psum | solution.py:197
  529.4 1.5 fusion.46
  (102 shorter events, 10.4 us)
Async XLA Ops:
  7.2 5.8 %copy-start = (bf16[512,1024]{1,0:T(8,128)(2,1)S(1)}, bf16[512,1024]{1,0:T(8,128)(2,1)}, u32[]{:S(2)}) copy-start(bf16[512,1024]{1,0:T(8,128)(2,1)} %param.19) | copy-start | bytes 3145732
  7.2 89.0 %all-reduce.14.cloned.1.call-start = ((), (), s32[]{:S(2)}) async-start(), calls=%async_computation.4 | async-start | bytes 132096 | tf_op jit(solution)/shard_map/psum | solution.py:102
  12.9 170.6 %all-reduce.8.cloned.1.call-start = ((), (), s32[]{:S(2)}) async-start(), calls=%async_computation | async-start | bytes 524288 | tf_op jit(solution)/shard_map/psum | solution.py:102
  14.8 246.6 %all-gather.3.cloned.1.call-start = ((), (), s32[]{:S(2)}) async-start(), calls=%async_computation.3 | async-start | bytes 4456448 | tf_op jit(solution)/shard_map/all_gather | solution.py:20
  97.7 100.6 %copy-start.4 = (bf16[64,128]{1,0:T(8,128)(2,1)}, bf16[64,128]{1,0:T(8,128)(2,1)S(1)}, u32[]{:S(2)}) copy-start(bf16[64,128]{1,0:T(8,128)(2,1)S(1)} %get-tuple-element.251) | copy-start | bytes 49156
  203.2 137.6 %all-reduce.10.cloned.1.call-start = ((), (), s32[]{:S(2)}) async-start(), calls=%async_computation.1 | async-start | bytes 131072 | tf_op jit(solution)/shard_map/psum | solution.py:182
  262.5 20.3 %copy-start.3 = (bf16[1024,512]{1,0:T(8,128)(2,1)S(1)}, bf16[1024,512]{1,0:T(8,128)(2,1)}, u32[]{:S(2)}) copy-start(bf16[1024,512]{1,0:T(8,128)(2,1)} %param.22) | copy-start | bytes 3145732
  262.5 21.3 %copy-start.5 = (bf16[512]{0:T(512)(128)(2,1)S(1)}, bf16[512]{0:T(512)(128)(2,1)}, u32[]{:S(2)}) copy-start(bf16[512]{0:T(512)(128)(2,1)} %param.23) | copy-start | bytes 3076
  262.5 78.3 %copy-start.2 = (bf16[64,512]{1,0:T(8,128)(2,1)S(1)}, bf16[64,512]{1,0:T(8,128)(2,1)}, u32[]{:S(2)}) copy-start(bf16[64,512]{1,0:T(8,128)(2,1)} %param.17) | copy-start | bytes 196612
  283.7 184.2 %all-reduce.16.cloned.1.call-start = ((), (), s32[]{:S(2)}) async-start(), calls=%async_computation.5 | async-start | bytes 1835008 | tf_op jit(solution)/shard_map/psum | solution.py:193
  375.1 3.8 copy-start.1
  380.5 148.9 %all-reduce.12.cloned.1.call-start = ((), (), s32[]{:S(2)}) async-start(), calls=%async_computation.2 | async-start | bytes 131072 | tf_op jit(solution)/shard_map/psum | solution.py:197
Sparse Core Ops, SparseCore 0:
  13.0 83.1 all-reduce.13
  99.7 83.7 all-reduce.7
  203.3 58.0 all-gather.2
  283.9 56.9 all-reduce.9
  380.6 87.3 all-reduce.15
  471.8 57.5 all-reduce.11
where the time goes:
time: 540 us; the launch traced here: 538 us
  waiting for transfers between devices  372 us (69%)
  blocking collectives  68.6 us (13%)
  matrix products  32.1 us (6%)
  other arithmetic  30.4 us (6%)
  local copies, waits for them, and re-layouts  19.3 us (4%)
  between operations  14.4 us (3%)
    psum x2, waiting for transfers between devices, body(): lax.psum((square_part, query_part, key_part, value_part), 'kvp')  151 us
    psum x1, waiting for transfers between devices, body(): lax.psum(up_part.astype(jnp.bfloat16), 'kvp').astype(jnp.float32)  87.4 us
    psum x1, waiting for transfers between devices, body(): lax.psum(attn_part.astype(jnp.bfloat16), 'head').astype(jnp.float32)  57 us
    psum x1, waiting for transfers between devices, body(): lax.psum(down_part.astype(jnp.bfloat16), 'head').astype(jnp.float32)  57 us
    all_gather x2, blocking collectives, joined(): gathered = jax.tree.map(lambda a: lax.all_gather(a, axis), part)  35.3 us
    psum x1, blocking collectives, body(): lax.psum(jnp.sum(residual_f * residual_f, axis=1, keepdims=True), 'kvp')  33.3 us
    all_gather x1, waiting for transfers between devices, joined(): gathered = jax.tree.map(lambda a: lax.all_gather(a, axis), part)  19.6 us
    dynamic_slice x33, local copies, waits for them, and re-layouts, take(): lax.dynamic_index_in_dim(a, source, 0, False)  15.9 us
  transfers between devices with their start and end apart: 6, of which 6 were waited for; matrix products, arithmetic and copies ran while one was open for 4% of the time, Pallas kernels for 0%

commit v1 on v0

v1 whole, which is shorter than its diff:
```python
import functools
import math

import jax
import jax.numpy as jnp
import numpy as np
from jax import lax
from jax.experimental import pallas as pl
from jax.experimental.pallas import tpu as pltpu
from jax.sharding import PartitionSpec as P

HD = 128
DRAFT = 4
BLOCK = 128
EPSILON = 1e-05
THETA_BASE = 500000.0
FLOOR = -1e30
LOG2E = math.log2(math.e)
EXP_SCALE = LOG2E / math.sqrt(HD)
UNROLL = 8
MESH = pl.DeviceIdType.MESH
F32 = jnp.float32
BF16 = jnp.bfloat16


def iota(shape, dim):
    return lax.broadcasted_iota(jnp.int32, shape, dim)


def dot(a, b):
    return jnp.dot(a, b, preferred_element_type=F32)


def dot_t(a, b):
    return lax.dot_general(a, b, (((1,), (1,)), ((), ())), preferred_element_type=F32)


def three_parts(x):
    high = x.astype(BF16).astype(F32)
    middle = (x - high).astype(BF16).astype(F32)
    return high, middle, x - high - middle


def kernel(
    nk,
    nh,
    width,
    hid_ref,
    gain_ref,
    post_ref,
    freq_ref,
    wq_hbm,
    wk_hbm,
    wv_hbm,
    wo_hbm,
    wg_hbm,
    wu_hbm,
    wd_hbm,
    keys_hbm,
    values_hbm,
    ctx_ref,
    req_ref,
    start_ref,
    next_ref,
    dkey_ref,
    dval_ref,
    wq,
    wk,
    wv,
    wo,
    wg,
    wu,
    wd,
    keys,
    values,
    hid8,
    send1,
    recv1,
    gath1,
    queries,
    scores,
    runs,
    tops,
    outs,
    sums,
    lasts,
    send2,
    recv2,
    gath2,
    send3,
    recv3,
    gath3,
    send4,
    recv4,
    gath4,
    send5,
    recv5,
    gath5,
    local_sem,
    ksend_sem,
    krecv_sem,
    hsend_sem,
    hrecv_sem,
):
    me_k = lax.axis_index("kvp")
    me_h = lax.axis_index("head")
    nm = nk // 2
    rows = 8 * nm
    me_m, me_c = me_k // 2, me_k % 2
    slots = keys.shape[0]
    db = hid_ref.shape[1]
    half = db // 2
    ff = wg.shape[1]
    fh = ff // 2
    fq = fh // 2

    first_copies = [
        pltpu.make_async_copy(src, dst, local_sem.at[i])
        for i, (src, dst) in enumerate([(wq_hbm, wq), (wk_hbm, wk), (wv_hbm, wv)])
    ]
    later_copies = [
        pltpu.make_async_copy(src, dst, local_sem.at[3 + i])
        for i, (src, dst) in enumerate(
            [(keys_hbm, keys), (values_hbm, values), (wo_hbm, wo), (wg_hbm, wg), (wu_hbm, wu), (wd_hbm, wd)]
        )
    ]
    for c in first_copies:
        c.start()

    barrier = pltpu.get_barrier_semaphore()

    def greet_k(k, _):
        pl.semaphore_signal(barrier, inc=1, device_id=(lax.rem(me_k + k, nk), me_h), device_id_type=MESH)
        return 0

    def greet_h(k, _):
        pl.semaphore_signal(barrier, inc=1, device_id=(me_k, lax.rem(me_h + k, nh)), device_id_type=MESH)
        return 0

    lax.fori_loop(1, nk, greet_k, 0)
    lax.fori_loop(1, nh, greet_h, 0)

    def kvp_copy(phase, k, src, dst):
        to = lax.rem(me_k + k, nk)
        return pltpu.make_async_remote_copy(
            src_ref=src,
            dst_ref=dst,
            send_sem=ksend_sem.at[phase, k],
            recv_sem=krecv_sem.at[phase, me_k],
            device_id=(to, me_h),
            device_id_type=MESH,
        )

    def kvp_wait(phase, source, ref):
        pltpu.make_async_remote_copy(
            src_ref=ref,
            dst_ref=ref,
            send_sem=ksend_sem.at[phase, 0],
            recv_sem=krecv_sem.at[phase, source],
            device_id=(source, me_h),
            device_id_type=MESH,
        ).wait_recv()

    def head_copy(phase, k, src, dst):
        to = lax.rem(me_h + k, nh)
        return pltpu.make_async_remote_copy(
            src_ref=src,
            dst_ref=dst,
            send_sem=hsend_sem.at[phase, k],
            recv_sem=hrecv_sem.at[phase, me_h],
            device_id=(me_k, to),
            device_id_type=MESH,
        )

    def head_wait(phase, source, ref):
        pltpu.make_async_remote_copy(
            src_ref=ref,
            dst_ref=ref,
            send_sem=hsend_sem.at[phase, 0],
            recv_sem=hrecv_sem.at[phase, source],
            device_id=(me_k, source),
            device_id_type=MESH,
        ).wait_recv()

    def kvp_scatter(phase, send, recv, only=None):
        def step(k, _):
            to = lax.rem(me_k + k, nk)
            copy = kvp_copy(phase, k, send.at[to // 2, to % 2], recv.at[me_k])
            if only is None:
                copy.start()
            else:
                pl.when(to % 2 == only)(copy.start)
            return 0

        lax.fori_loop(1, nk, step, 0)

    def kvp_gather(phase, gath):
        def step(k, _):
            kvp_copy(phase, k, gath.at[me_m, me_c], gath.at[me_m, me_c]).start()
            return 0

        lax.fori_loop(1, nk, step, 0)

    def kvp_gather_wait(phase, gath):
        def step(k, _):
            source = lax.rem(me_k + k, nk)
            kvp_wait(phase, source, gath.at[source // 2, source % 2])
            return 0

        lax.fori_loop(1, nk, step, 0)

    def kvp_reduce(phase, send, recv):
        def step(k, total):
            source = lax.rem(me_k + k, nk)
            kvp_wait(phase, source, recv.at[source])
            return total + recv[source].astype(F32)

        return lax.fori_loop(1, nk, step, send[me_m, me_c].astype(F32))

    def head_sum(phase, part, send, recv):
        parts = part.reshape(nh, 8, db)
        send[...] = jnp.concatenate([parts[:, :, :half], parts[:, :, half:]], axis=1).astype(BF16)

        def scatter(k, _):
            to = lax.rem(me_h + k, nh)
            head_copy(phase, k, send.at[to], recv.at[me_h]).start()
            return 0

        lax.fori_loop(1, nh, scatter, 0)

        def step(k, total):
            source = lax.rem(me_h + k, nh)
            head_wait(phase, source, recv.at[source])
            return total + recv[source].astype(F32)

        return lax.fori_loop(1, nh, step, send[me_h].astype(F32))

    def head_gather(phase, gath):
        def step(k, _):
            head_copy(phase, k, gath.at[me_h], gath.at[me_h]).start()
            return 0

        lax.fori_loop(1, nh, step, 0)

        def wait(k, _):
            source = lax.rem(me_h + k, nh)
            head_wait(phase, source, gath.at[source])
            return 0

        lax.fori_loop(1, nh, wait, 0)

    def folded(x):
        return jnp.concatenate([x[:, : x.shape[1] // 2], x[:, x.shape[1] // 2 :]], axis=0)

    hidden = hid_ref[...].astype(F32)
    hid8[...] = hidden.reshape(nh, 8, db)
    scaled = (hidden * gain_ref[...].astype(F32)).astype(BF16)
    square = jnp.sum(hidden * hidden, axis=1, keepdims=True)
    lane = iota((rows, HD), 1)

    def square_tile(column):
        high, middle, low = three_parts(jnp.broadcast_to(column, (rows, HD)))
        return jnp.where(lane == 0, high, jnp.where(lane == 1, middle, jnp.where(lane == 2, low, 0.0)))

    square_in = square_tile(square)
    for c in first_copies:
        c.wait()
    for c in later_copies:
        c.start()
    key_part = dot(scaled, wk[...])
    value_part = dot(scaled, wv[...])
    for c in range(2):
        query_part = dot(scaled, wq[:, c * 512 : (c + 1) * 512])
        upper = query_part[:, :384]
        lower = jnp.concatenate([query_part[:, 384:], value_part if c else key_part, square_in], axis=1)
        send1[:, c] = jnp.concatenate([upper.reshape(nm, 8, 384), lower.reshape(nm, 8, 384)], axis=1).astype(BF16)

    pl.semaphore_wait(barrier, nk + nh - 2)
    kvp_scatter(0, send1, recv1)

    eight = iota((8, HD), 0)
    lane8 = iota((8, HD), 1)
    position = jnp.where(eight < DRAFT, ctx_ref[2 * me_m], ctx_ref[2 * me_m + 1]) + eight % DRAFT
    angle = position.astype(F32) * freq_ref[...]
    cosine = jnp.cos(angle)
    sine = jnp.sin(angle)
    sine = jnp.where(lane8 < HD // 2, -sine, sine)

    def find_last(s, last):
        return jnp.where(lane8 == req_ref[s], s, last)

    lasts[...] = lax.fori_loop(0, slots, find_last, jnp.full((8, HD), -1, jnp.int32), unroll=8)

    total = kvp_reduce(0, send1, recv1)
    square_sum = jnp.sum(total[8:, 256:], axis=1, keepdims=True)
    inverse = lax.rsqrt(square_sum / width + EPSILON)
    tiles = [total[:8, :128], total[:8, 128:256], total[:8, 256:], total[8:, :128], total[8:, 128:256]]
    tiles = [t * inverse for t in tiles]
    rotated = [t * cosine + pltpu.roll(t, HD // 2, 1) * sine for t in tiles]
    low_rows = eight < DRAFT

    def swap(x):
        return pltpu.roll(x, DRAFT, 0)

    def first_of(a, b):
        return jnp.where(low_rows, a, swap(b))

    def second_of(a, b):
        return jnp.where(low_rows, swap(a), b)

    q0, q1, q2, q3 = rotated[:4]
    pair = jnp.where(me_c == 0, rotated[4], tiles[4])
    gath1[me_m, me_c, 0] = jnp.concatenate([first_of(q0, q1), first_of(q2, q3)], axis=0).astype(BF16)
    gath1[me_m, me_c, 1] = jnp.concatenate([second_of(q0, q1), second_of(q2, q3)], axis=0).astype(BF16)
    gath1[me_m, me_c, 2] = jnp.concatenate([pair, jnp.zeros_like(pair)], axis=0).astype(BF16)
    kvp_gather(1, gath1)
    kvp_gather_wait(1, gath1)
    for m in range(nm):
        for s in range(2):
            queries[2 * m + s, :16] = gath1[m, 0, s]
            queries[2 * m + s, 16:] = gath1[m, 1, s]
    drafts = [
        jnp.concatenate([gath1[m, c, 2].astype(F32)[:8] for m in range(nm)], axis=0).astype(BF16) for c in range(2)
    ]
    dkey_ref[...] = drafts[0]
    dval_ref[...] = drafts[1]

    later_copies[0].wait()
    token = iota((32, BLOCK), 1)

    def previous(s):
        return req_ref[jnp.maximum(s - 1, 0)]

    def score_step(i, run):
        for u in range(UNROLL):
            s = i * UNROLL + u
            r = req_ref[s]
            safe = jnp.maximum(r, 0)
            live = jnp.where(r >= 0, ctx_ref[safe] - start_ref[s], 0)
            part = jnp.where(token < live, dot_t(queries[safe], keys[s]), FLOOR)
            scores[s] = part
            run = jnp.maximum(part, jnp.where(r == previous(s), run, FLOOR))
            runs[s] = run
        return run

    floor_tile = jnp.full((32, BLOCK), FLOOR, F32)
    lax.fori_loop(0, slots // UNROLL, score_step, floor_tile)
    last_of = [jnp.max(jnp.where(lane8 == b, lasts[...], -1)) for b in range(nk)]
    for b in range(nk):
        run = runs[jnp.maximum(last_of[b], 0)]
        top = jnp.max(run, axis=1, keepdims=True)
        tops[b] = jnp.where(last_of[b] >= 0, jnp.broadcast_to(top, (32, BLOCK)), FLOOR)

    later_copies[1].wait()

    def value_step(i, carry):
        sum_run, out_run = carry
        for u in range(UNROLL):
            s = i * UNROLL + u
            r = req_ref[s]
            keep = jnp.where(r == previous(s), 1.0, 0.0).astype(F32)
            weight = jnp.exp2((scores[s] - tops[jnp.maximum(r, 0)]) * EXP_SCALE)
            sum_run = sum_run * keep + weight
            out_run = out_run * keep + dot(weight.astype(BF16), values[s])
            sums[s] = sum_run
            outs[s] = out_run
        return sum_run, out_run

    zero_tile = jnp.zeros((32, BLOCK), F32)
    lax.fori_loop(0, slots // UNROLL, value_step, (zero_tile, zero_tile))

    lane32 = iota((32, HD), 1)
    stats = zero_tile
    totals = []
    for b in range(nk):
        at = jnp.maximum(last_of[b], 0)
        here = last_of[b] >= 0
        out = jnp.where(here, outs[at], 0.0)
        column = jnp.sum(sums[at], axis=1, keepdims=True)
        totals.append(jnp.where(here, jnp.broadcast_to(column, (32, HD)), 0.0))
        for c in range(2):
            send2[b // 2, c, 16 * (b % 2) : 16 * (b % 2) + 16, :] = out[16 * c : 16 * c + 16].astype(BF16)
    for m in range(nm):
        for c in range(2):
            j = 2 * m + c
            part = slice(16 * c, 16 * c + 16)
            top = jnp.concatenate([tops[2 * m, part], tops[2 * m + 1, part]], axis=0)
            summed = jnp.concatenate([totals[2 * m][part], totals[2 * m + 1][part]], axis=0)
            stats = jnp.where(lane32 // 8 == j, jnp.where(lane32 % 8 < 3, top, summed), stats)
    high, middle, low = three_parts(stats)
    kind = lane32 % 8
    stats = jnp.where(
        kind % 3 == 0, high, jnp.where(kind % 3 == 1, middle, low)
    )
    stats = jnp.where(kind < 6, stats, 0.0)
    turned = jnp.concatenate([stats, jnp.zeros((HD - 32, HD), F32)], axis=0).T
    for m in range(nm):
        for c in range(2):
            j = 2 * m + c
            tile = jnp.concatenate([turned[8 * j : 8 * j + 8], jnp.zeros((8, HD), F32)], axis=0)
            send2[m, c, 32:48, :] = tile.astype(BF16)
    kvp_scatter(2, send2, recv2)

    mine = jnp.concatenate([gath1[me_m, me_c, 0], gath1[me_m, me_c, 1]], axis=0)
    draft_score = dot_t(mine, gath1[me_m, 0, 2])
    row16, col16 = iota((32, 16), 0), iota((32, 16), 1)
    seen = (col16 // DRAFT == row16 // 16) & (col16 % DRAFT <= row16 % DRAFT)
    draft_score = jnp.where(seen, draft_score, FLOOR)
    draft_top = jnp.max(draft_score, axis=1, keepdims=True)
    draft_weight = jnp.where(seen, jnp.exp2((draft_score - draft_top) * EXP_SCALE), 0.0)
    draft_sum = jnp.sum(draft_weight, axis=1, keepdims=True)
    draft_out = dot(draft_weight.astype(BF16), gath1[me_m, 1, 2])

    recv2[me_k] = send2[me_m, me_c]

    def wait2(k, _):
        source = lax.rem(me_k + k, nk)
        kvp_wait(2, source, recv2.at[source])
        return 0

    lax.fori_loop(1, nk, wait2, 0)
    every = [recv2[i, 32:48, :].astype(F32)[:8] for i in range(nk)]
    every = jnp.concatenate(every + [jnp.zeros((8, HD), F32)] * (HD // 8 - nk), axis=0)
    turned = every.T[:32]
    joined = turned + pltpu.roll(turned, HD - 1, 1) + pltpu.roll(turned, HD - 2, 1)
    own_lane = (lane32 % 8 == 0) & (lane32 < 8 * nk)
    peak = jnp.max(jnp.where(own_lane, joined, FLOOR), axis=1, keepdims=True)
    peak = jnp.maximum(peak, draft_top)
    factor = jnp.where(own_lane, jnp.exp2((joined - peak) * EXP_SCALE), 0.0)
    whole = jnp.where(own_lane, factor * pltpu.roll(joined, HD - 3, 1), 0.0)
    draft_factor = jnp.exp2((draft_top - peak) * EXP_SCALE)
    whole = jnp.sum(whole, axis=1, keepdims=True) + draft_sum * draft_factor
    factor = factor / whole
    mixed = draft_out * (draft_factor / whole)
    for i in range(nk):
        mixed = mixed + recv2[i, :32, :].astype(F32) * factor[:, 8 * i : 8 * i + 1]
    a0, a1, b0, b1 = mixed[:8], mixed[8:16], mixed[16:24], mixed[24:]
    h0, h1 = first_of(a0, b0), second_of(a0, b0)
    h2, h3 = first_of(a1, b1), second_of(a1, b1)
    gath2[me_m, me_c] = jnp.concatenate(
        [jnp.concatenate([h0, h1], axis=1), jnp.concatenate([h2, h3], axis=1)], axis=0
    ).astype(BF16)
    kvp_gather(3, gath2)
    later_copies[2].wait()
    kvp_gather_wait(3, gath2)

    attn_part = jnp.zeros((rows, db), F32)
    for c in range(2):
        for g in range(2):
            piece = jnp.concatenate(
                [gath2[m, c].astype(F32)[8 * g : 8 * g + 8] for m in range(nm)], axis=0
            ).astype(BF16)
            attn_part += dot(piece, wo[512 * c + 256 * g : 512 * c + 256 * g + 256, :])
    attn = head_sum(0, attn_part, send3, recv3)
    gath3[me_h] = (folded(hid8[me_h]) + attn).astype(BF16)
    head_gather(1, gath3)

    def unfolded(gath):
        pieces = [gath[h].astype(F32) for h in range(nh)]
        return jnp.concatenate(
            [jnp.concatenate([p[:8] for p in pieces], axis=0), jnp.concatenate([p[8:] for p in pieces], axis=0)],
            axis=1,
        )

    residual = unfolded(gath3)
    square_out = square_tile(jnp.sum(residual * residual, axis=1, keepdims=True)).reshape(nm, 8, HD)
    normed = (residual * post_ref[...].astype(F32)).astype(BF16)
    chunk = 256 if fh % 256 == 0 else 128
    later_copies[3].wait()
    later_copies[4].wait()
    for c in range(2):

        def up_step(i, _):
            at = pl.multiple_of(c * fh + i * chunk, chunk)
            gate = dot(normed, wg[:, pl.ds(at, chunk)]).reshape(nm, 8, chunk)
            up = dot(normed, wu[:, pl.ds(at, chunk)]).reshape(nm, 8, chunk)
            send4[:, c, :, pl.ds(pl.multiple_of(i * chunk, chunk), chunk)] = jnp.concatenate(
                [gate, up], axis=1
            ).astype(BF16)
            return 0

        lax.fori_loop(0, fh // chunk, up_step, 0)
        send4[:, c, :, fh:] = jnp.concatenate([square_out, jnp.zeros_like(square_out)], axis=1).astype(BF16)
        kvp_scatter(4, send4, recv4, only=c)
    total = kvp_reduce(4, send4, recv4)
    square_sum = jnp.sum(total[:8, fh:], axis=1, keepdims=True)
    inverse = lax.rsqrt(square_sum / width + EPSILON)
    gate = total[:8, :fh] * inverse
    up = total[8:, :fh] * inverse
    middle = gate / (1.0 + jnp.exp(-gate)) * up
    gath4[me_m, me_c] = folded(middle).astype(BF16)
    kvp_gather(5, gath4)
    later_copies[5].wait()
    kvp_gather_wait(5, gath4)
    down_part = jnp.zeros((rows, db), F32)
    for c in range(2):
        for g in range(2):
            piece = jnp.concatenate(
                [gath4[m, c].astype(F32)[8 * g : 8 * g + 8] for m in range(nm)], axis=0
            ).astype(BF16)
            at = fh * c + fq * g
            down_part += dot(piece, wd[at : at + fq, :])
    down = head_sum(2, down_part, send5, recv5)
    gath5[me_h] = (gath3[me_h].astype(F32) + down).astype(BF16)
    head_gather(3, gath5)
    next_ref[...] = unfolded(gath5).astype(BF16)

    def kvp_done(k, _):
        for phase, ref in ((0, recv1), (2, recv2), (4, recv4)):
            kvp_copy(phase, k, ref.at[0], ref.at[0]).wait_send()
        for phase, ref in ((1, gath1), (3, gath2), (5, gath4)):
            kvp_copy(phase, k, ref.at[0, 0], ref.at[0, 0]).wait_send()
        return 0

    lax.fori_loop(1, nk, kvp_done, 0)

    def head_done(k, _):
        for phase, ref in ((0, recv3), (1, gath3), (2, recv5), (3, gath5)):
            head_copy(phase, k, ref.at[0], ref.at[0]).wait_send()
        return 0

    lax.fori_loop(1, nh, head_done, 0)


def body(
    nk,
    nh,
    hidden_in,
    norm_gain,
    w_query,
    w_key,
    w_value,
    w_out,
    post_gain,
    w_gate,
    w_up,
    w_down,
    cache_keys,
    cache_values,
    context_len,
    slot_request,
    slot_start,
):
    rows, db = hidden_in.shape
    nm = nk // 2
    slots = cache_keys.shape[0]
    fh = w_gate.shape[1] // 2
    exponent = np.arange(HD // 2, dtype=np.float32) * np.float32(2.0 / HD)
    frequency = (THETA_BASE ** (-exponent.astype(np.float64))).astype(np.float32)
    frequency = jnp.asarray(np.concatenate([frequency, frequency])[None, :])
    vmem = pl.BlockSpec(memory_space=pltpu.VMEM)
    hbm = pl.BlockSpec(memory_space=pl.ANY)
    smem = pl.BlockSpec(memory_space=pltpu.SMEM)
    scratch = [
        pltpu.VMEM(w.shape, BF16)
        for w in (w_query, w_key, w_value, w_out, w_gate, w_up, w_down, cache_keys, cache_values)
    ]
    scratch += [
        pltpu.VMEM((nh, 8, db), F32),
        pltpu.VMEM((nm, 2, 16, 384), BF16),
        pltpu.VMEM((nk, 16, 384), BF16),
        pltpu.VMEM((nm, 2, 3, 16, HD), BF16),
        pltpu.VMEM((nk, 32, HD), BF16),
        pltpu.VMEM((slots, 32, BLOCK), F32),
        pltpu.VMEM((slots, 32, BLOCK), F32),
        pltpu.VMEM((nk, 32, BLOCK), F32),
        pltpu.VMEM((slots, 32, HD), F32),
        pltpu.VMEM((slots, 32, BLOCK), F32),
        pltpu.VMEM((8, HD), jnp.int32),
        pltpu.VMEM((nm, 2, 48, HD), BF16),
        pltpu.VMEM((nk, 48, HD), BF16),
        pltpu.VMEM((nm, 2, 16, 256), BF16),
        pltpu.VMEM((nh, 16, db // 2), BF16),
        pltpu.VMEM((nh, 16, db // 2), BF16),
        pltpu.VMEM((nh, 16, db // 2), BF16),
        pltpu.VMEM((nm, 2, 16, fh + HD), BF16),
        pltpu.VMEM((nk, 16, fh + HD), BF16),
        pltpu.VMEM((nm, 2, 16, fh // 2), BF16),
        pltpu.VMEM((nh, 16, db // 2), BF16),
        pltpu.VMEM((nh, 16, db // 2), BF16),
        pltpu.VMEM((nh, 16, db // 2), BF16),
        pltpu.SemaphoreType.DMA((9,)),
        pltpu.SemaphoreType.DMA((6, nk)),
        pltpu.SemaphoreType.DMA((6, nk)),
        pltpu.SemaphoreType.DMA((4, nh)),
        pltpu.SemaphoreType.DMA((4, nh)),
    ]
    weight_items = sum(w.size for w in (w_query, w_key, w_value, w_out, w_gate, w_up, w_down))
    return pl.pallas_call(
        functools.partial(kernel, nk, nh, db * nk),
        out_shape=(
            jax.ShapeDtypeStruct((rows, db), BF16),
            jax.ShapeDtypeStruct((rows, HD), BF16),
            jax.ShapeDtypeStruct((rows, HD), BF16),
        ),
        in_specs=[vmem] * 4 + [hbm] * 9 + [smem] * 3,
        out_specs=(vmem, vmem, vmem),
        scratch_shapes=scratch,
        compiler_params=pltpu.CompilerParams(
            collective_id=0, has_side_effects=True, vmem_limit_bytes=56 * 1024 * 1024
        ),
        cost_estimate=pl.CostEstimate(
            flops=2 * rows * weight_items + 4 * slots * 32 * BLOCK * HD,
            bytes_accessed=2 * (weight_items + 2 * cache_keys.size),
            transcendentals=slots * 32 * BLOCK,
        ),
    )(
        hidden_in,
        norm_gain.reshape(1, db),
        post_gain.reshape(1, db),
        frequency,
        w_query,
        w_key,
        w_value,
        w_out,
        w_gate,
        w_up,
        w_down,
        cache_keys,
        cache_values,
        context_len,
        slot_request,
        slot_start,
    )


def solution(mesh):
    return jax.shard_map(
        functools.partial(body, mesh.shape["kvp"], mesh.shape["head"]),
        mesh=mesh,
        in_specs=(
            P(None, "kvp"),
            P("kvp"),
            P("kvp", "head"),
            P("kvp", "head"),
            P("kvp", "head"),
            P("head", "kvp"),
            P("kvp"),
            P("kvp", "head"),
            P("kvp", "head"),
            P("head", "kvp"),
            P("kvp", None, "head"),
            P("kvp", None, "head"),
            P(),
            P("kvp"),
            P("kvp"),
        ),
        out_specs=(P(None, "kvp"), P(None, "head"), P(None, "head")),
        check_vma=False,
    )
```

time: 540 us -> 91.5 us (0.17)
  waiting for transfers between devices: 372 us -> 0 us
  Pallas kernels: 0 us -> 83.9 us
  blocking collectives: 68.6 us -> 0 us
  matrix products: 32.1 us -> 0 us
  other arithmetic: 30.4 us -> 0 us
  between operations: 14.4 us -> 0.64 us
  local copies, waits for them, and re-layouts: 19.3 us -> 6.64 us
    psum x5 -> x0, waiting for transfers between devices: 353 us -> none  [the longest x2 151 us: body(): lax.psum((square_part, query_part, key_part, value_part), 'kvp')]
    pallas_call x0 -> x1, Pallas kernels: none -> 83.9 us  [body(): pl.pallas_call(functools.partial(kernel, nk, nh, db * nk), out_shape=(jax...]
    all_gather x2 -> x0, blocking collectives: 35.3 us -> none  [joined(): gathered = jax.tree.map(lambda a: lax.all_gather(a, axis), part)]
    psum x1 -> x0, blocking collectives: 33.3 us -> none  [body(): lax.psum(jnp.sum(residual_f * residual_f, axis=1, keepdims=True), 'kvp')]
    dot_general x12 -> x0, matrix products: 32.1 us -> none  [the longest x1 6.91 us: body(): jnp.einsum('skqd,stkd->skqt', chosen, slot_keys, preferred_element_type=j...]
    all_gather x1 -> x0, waiting for transfers between devices: 19.6 us -> none  [joined(): gathered = jax.tree.map(lambda a: lax.all_gather(a, axis), part)]
    dynamic_slice x33 -> x0, local copies, waits for them, and re-layouts: 15.9 us -> none  [take(): lax.dynamic_index_in_dim(a, source, 0, False)]
    select_n x2 -> x0, other arithmetic: 10.5 us -> none  [the longest x1 10.5 us: body(): limits = jnp.take(context_len, safe_req)]
  transfers between devices with their start and end apart: 6 -> 0, of which waited for: 6 -> 0; matrix products, arithmetic and copies ran while one was open for 4% -> 0% of each run, Pallas kernels for 0% -> 0%
where the time goes in v1:
time: 91.5 us; the launch traced here: 91.1 us
  Pallas kernels  83.9 us (92%)
  local copies, waits for them, and re-layouts  6.64 us (7%)
    pallas_call x1, Pallas kernels, body(): pl.pallas_call(functools.partial(kernel, nk, nh, db * nk), out_shape=(jax...  83.9 us
    unnamed x3, local copies, waits for them, and re-layouts  4.12 us

profile of v1, /device:TPU:1, one launch (start us, length us, event | category | flops | bytes accessed | tf_op | source)
XLA Modules:
  0.0 91.1 jit_solution(16517472150854533098)
XLA Ops:
  0.6 1.3 %reshape.12.gain_ref = bf16[1,512]{1,0:T(2,128)(2,1)} reshape(bf16[512]{0:T(512)(128)(2,1)} %param.17) | data formatting | bytes 2048 | tf_op jit(solution)/shard_map/reshape | solution.py:609
  1.9 1.3 %reshape.13.post_ref = bf16[1,512]{1,0:T(2,128)(2,1)} reshape(bf16[512]{0:T(512)(128)(2,1)} %param.22) | data formatting | bytes 2048 | tf_op jit(solution)/shard_map/reshape | solution.py:610
  3.1 83.9 %shard_map.175 = (bf16[64,512]{1,0:T(8,128)(2,1)}, bf16[64,128]{1,0:T(8,128)(2,1)}, bf16[64,128]{1,0:T(8,128)(2,1)}) custom-call(bf16[64,512]{1,0:T(8,128)(2,1)} %hid_ref.1, bf16[1,512]{1,0:T(2,128)(2,1)} %reshape.12.gain_ref, bf16[1,512]{1,0:T(2,128)(2,1)} %reshape.13.post_ref, f32[1,128]{1,0:T(1,128)} %constant.2.clone.freq_ref, bf16[512,1024]{1,0:T(8,128)(2,1)} %wq_hbm.1, ...), custom_call_target="tpu_custom_call" | custom-call | flops 1191182336 | bytes 23855104 | tf_op jit(solution)/shard_map/pallas_call | solution.py:589
  87.0 1.5 %copy.22 = bf16[64,512]{1,0:T(8,128)(2,1)} copy(bf16[64,512]{1,0:T(8,128)(2,1)} %get-tuple-element.6) | data formatting | bytes 131072
  88.5 1.3 %copy.23 = bf16[64,128]{1,0:T(8,128)(2,1)} copy(bf16[64,128]{1,0:T(8,128)(2,1)} %get-tuple-element.7) | data formatting | bytes 32768
  89.8 1.3 %copy.24 = bf16[64,128]{1,0:T(8,128)(2,1)} copy(bf16[64,128]{1,0:T(8,128)(2,1)} %get-tuple-element.8) | data formatting | bytes 32768

commit v2 on v1

--- a/solution.py
+++ b/solution.py
@@ -17,7 +17,7 @@
 FLOOR = -1e30
 LOG2E = math.log2(math.e)
 EXP_SCALE = LOG2E / math.sqrt(HD)
-UNROLL = 8
+UNROLL = 32
 MESH = pl.DeviceIdType.MESH
 F32 = jnp.float32
 BF16 = jnp.bfloat16
@@ -39,6 +39,20 @@
     high = x.astype(BF16).astype(F32)
     middle = (x - high).astype(BF16).astype(F32)
     return high, middle, x - high - middle
+
+
+def pieces_of(columns):
+    size = 512 if columns > 512 else columns // 2
+    return [(at, min(size, columns - at)) for at in range(0, columns, size)]
+
+
+def hand_on(*refs):
+    sources, targets, sem = refs[:3], refs[3:6], refs[6]
+    copies = [pltpu.make_async_copy(a, b, sem.at[i]) for i, (a, b) in enumerate(zip(sources, targets))]
+    for copy in copies:
+        copy.start()
+    for copy in copies:
+        copy.wait()
 
 
 def kernel(
@@ -73,7 +87,7 @@
     wd,
     keys,
     values,
-    hid8,
+    hidden_halves,
     send1,
     recv1,
     gath1,
@@ -87,15 +101,17 @@
     send2,
     recv2,
     gath2,
-    send3,
-    recv3,
-    gath3,
+    core3,
+    along3,
+    resid,
+    send_sq,
+    recv_sq,
     send4,
     recv4,
     gath4,
-    send5,
-    recv5,
-    gath5,
+    core5,
+    along5,
+    final,
     local_sem,
     ksend_sem,
     krecv_sem,
@@ -105,6 +121,13 @@
     me_k = lax.axis_index("kvp")
     me_h = lax.axis_index("head")
     nm = nk // 2
+    nz = nh // 2
+    me_z, core = me_h // 2, me_h % 2
+    twin = me_h + 1 - 2 * core
+
+    def along_z(k):
+        return lax.rem(me_z + k, nz) * 2 + core
+
     rows = 8 * nm
     me_m, me_c = me_k // 2, me_k % 2
     slots = keys.shape[0]
@@ -112,7 +135,10 @@
     half = db // 2
     ff = wg.shape[1]
     fh = ff // 2
-    fq = fh // 2
+    pieces = pieces_of(fh)
+
+    started = []
+    sent = []
 
     first_copies = [
         pltpu.make_async_copy(src, dst, local_sem.at[i])
@@ -124,6 +150,9 @@
             [(keys_hbm, keys), (values_hbm, values), (wo_hbm, wo), (wg_hbm, wg), (wu_hbm, wu), (wd_hbm, wd)]
         )
     ]
+    def arrive(i):
+        later_copies[i].wait()
+
     for c in first_copies:
         c.start()
 
@@ -133,12 +162,9 @@
         pl.semaphore_signal(barrier, inc=1, device_id=(lax.rem(me_k + k, nk), me_h), device_id_type=MESH)
         return 0
 
-    def greet_h(k, _):
-        pl.semaphore_signal(barrier, inc=1, device_id=(me_k, lax.rem(me_h + k, nh)), device_id_type=MESH)
-        return 0
-
     lax.fori_loop(1, nk, greet_k, 0)
-    lax.fori_loop(1, nh, greet_h, 0)
+    for to in [twin] + [along_z(k) for k in range(1, nz)]:
+        pl.semaphore_signal(barrier, inc=1, device_id=(me_k, to), device_id_type=MESH)
 
     def kvp_copy(phase, k, src, dst):
         to = lax.rem(me_k + k, nk)
@@ -161,42 +187,32 @@
             device_id_type=MESH,
         ).wait_recv()
 
-    def head_copy(phase, k, src, dst):
-        to = lax.rem(me_h + k, nh)
+    def head_copy(sem, to, src, dst):
         return pltpu.make_async_remote_copy(
             src_ref=src,
             dst_ref=dst,
-            send_sem=hsend_sem.at[phase, k],
-            recv_sem=hrecv_sem.at[phase, me_h],
+            send_sem=hsend_sem.at[sem],
+            recv_sem=hrecv_sem.at[sem],
             device_id=(me_k, to),
             device_id_type=MESH,
         )
 
-    def head_wait(phase, source, ref):
-        pltpu.make_async_remote_copy(
-            src_ref=ref,
-            dst_ref=ref,
-            send_sem=hsend_sem.at[phase, 0],
-            recv_sem=hrecv_sem.at[phase, source],
-            device_id=(me_k, source),
-            device_id_type=MESH,
-        ).wait_recv()
-
-    def kvp_scatter(phase, send, recv, only=None):
+    def kvp_scatter(phase, send, recv):
+        started.append((kvp_copy, phase, recv.at[0], range(1, nk)))
+
         def step(k, _):
             to = lax.rem(me_k + k, nk)
-            copy = kvp_copy(phase, k, send.at[to // 2, to % 2], recv.at[me_k])
-            if only is None:
-                copy.start()
-            else:
-                pl.when(to % 2 == only)(copy.start)
+            kvp_copy(phase, k, send.at[to // 2, to % 2], recv.at[me_k]).start()
             return 0
 
         lax.fori_loop(1, nk, step, 0)
 
     def kvp_gather(phase, gath):
+        mine = gath.at[me_m, me_c]
+        started.append((kvp_copy, phase, mine, range(1, nk)))
+
         def step(k, _):
-            kvp_copy(phase, k, gath.at[me_m, me_c], gath.at[me_m, me_c]).start()
+            kvp_copy(phase, k, mine, mine).start()
             return 0
 
         lax.fori_loop(1, nk, step, 0)
@@ -217,44 +233,55 @@
 
         return lax.fori_loop(1, nk, step, send[me_m, me_c].astype(F32))
 
-    def head_sum(phase, part, send, recv):
-        parts = part.reshape(nh, 8, db)
-        send[...] = jnp.concatenate([parts[:, :, :half], parts[:, :, half:]], axis=1).astype(BF16)
-
-        def scatter(k, _):
-            to = lax.rem(me_h + k, nh)
-            head_copy(phase, k, send.at[to], recv.at[me_h]).start()
-            return 0
-
-        lax.fori_loop(1, nh, scatter, 0)
-
-        def step(k, total):
-            source = lax.rem(me_h + k, nh)
-            head_wait(phase, source, recv.at[source])
-            return total + recv[source].astype(F32)
-
-        return lax.fori_loop(1, nh, step, send[me_h].astype(F32))
-
-    def head_gather(phase, gath):
-        def step(k, _):
-            head_copy(phase, k, gath.at[me_h], gath.at[me_h]).start()
-            return 0
-
-        lax.fori_loop(1, nh, step, 0)
-
-        def wait(k, _):
-            source = lax.rem(me_h + k, nh)
-            head_wait(phase, source, gath.at[source])
-            return 0
-
-        lax.fori_loop(1, nh, wait, 0)
+    def halves(x):
+        return x[:, :half], x[:, half:]
+
+    def own_half(x):
+        left, right = halves(x)
+        return jnp.where(core == 0, left, right), jnp.where(core == 0, right, left)
+
+    def head_sum(base, part, swap_ref, along_ref):
+        own, other = own_half(part)
+        swap_ref[0] = other.astype(BF16)
+        swapped = head_copy(base, twin, swap_ref.at[0], swap_ref.at[1])
+        swapped.start()
+        sent.append(swapped)
+        swapped.wait_recv()
+        along_ref[0] = (own + swap_ref[1].astype(F32)).astype(BF16)
+        copies = [head_copy(base + k, along_z(k), along_ref.at[0], along_ref.at[k]) for k in range(1, nz)]
+        for copy in copies:
+            copy.start()
+        sent.extend(copies)
+        for copy in copies:
+            copy.wait_recv()
+        total = jnp.zeros((rows, half), F32)
+        for z in range(nz):
+            total = total + along_ref[lax.rem(me_z - z + nz, nz)].astype(F32)
+        return total
+
+    def share_half(sem, ref):
+        copy = head_copy(sem, twin, ref.at[core], ref.at[core])
+        copy.start()
+        sent.append(copy)
+        copy.wait_recv()
+
+    def finish():
+        for copy in sent:
+            copy.wait_send()
+        for copy, phase, ref, keys_of in started:
+
+            def done(k, _, copy=copy, phase=phase, ref=ref):
+                copy(phase, k, ref, ref).wait_send()
+                return 0
+
+            lax.fori_loop(keys_of.start, keys_of.stop, done, 0)
 
     def folded(x):
         return jnp.concatenate([x[:, : x.shape[1] // 2], x[:, x.shape[1] // 2 :]], axis=0)
 
     hidden = hid_ref[...].astype(F32)
-    hid8[...] = hidden.reshape(nh, 8, db)
-    scaled = (hidden * gain_ref[...].astype(F32)).astype(BF16)
+    hidden_halves[0], hidden_halves[1] = halves(hidden)
+    scaled = (hidden * gain_ref[...].astype(F32).reshape(1, db)).astype(BF16)
     square = jnp.sum(hidden * hidden, axis=1, keepdims=True)
     lane = iota((rows, HD), 1)
 
@@ -275,7 +302,7 @@
         lower = jnp.concatenate([query_part[:, 384:], value_part if c else key_part, square_in], axis=1)
         send1[:, c] = jnp.concatenate([upper.reshape(nm, 8, 384), lower.reshape(nm, 8, 384)], axis=1).astype(BF16)
 
-    pl.semaphore_wait(barrier, nk + nh - 2)
+    pl.semaphore_wait(barrier, nk + nz - 1)
     kvp_scatter(0, send1, recv1)
 
     eight = iota((8, HD), 0)
@@ -325,7 +352,7 @@
     dkey_ref[...] = drafts[0]
     dval_ref[...] = drafts[1]
 
-    later_copies[0].wait()
+    arrive(0)
     token = iota((32, BLOCK), 1)
 
     def previous(s):
@@ -351,7 +378,7 @@
         top = jnp.max(run, axis=1, keepdims=True)
         tops[b] = jnp.where(last_of[b] >= 0, jnp.broadcast_to(top, (32, BLOCK)), FLOOR)
 
-    later_copies[1].wait()
+    arrive(1)
 
     def value_step(i, carry):
         sum_run, out_run = carry
@@ -441,7 +468,7 @@
         [jnp.concatenate([h0, h1], axis=1), jnp.concatenate([h2, h3], axis=1)], axis=0
     ).astype(BF16)
     kvp_gather(3, gath2)
-    later_copies[2].wait()
+    arrive(2)
     kvp_gather_wait(3, gath2)
 
     attn_part = jnp.zeros((rows, db), F32)
@@ -451,75 +478,87 @@
                 [gath2[m, c].astype(F32)[8 * g : 8 * g + 8] for m in range(nm)], axis=0
             ).astype(BF16)
             attn_part += dot(piece, wo[512 * c + 256 * g : 512 * c + 256 * g + 256, :])
-    attn = head_sum(0, attn_part, send3, recv3)
-    gath3[me_h] = (folded(hid8[me_h]) + attn).astype(BF16)
-    head_gather(1, gath3)
-
-    def unfolded(gath):
-        pieces = [gath[h].astype(F32) for h in range(nh)]
-        return jnp.concatenate(
-            [jnp.concatenate([p[:8] for p in pieces], axis=0), jnp.concatenate([p[8:] for p in pieces], axis=0)],
-            axis=1,
-        )
-
-    residual = unfolded(gath3)
+    attn = head_sum(0, attn_part, core3, along3)
+    resid[core] = (hidden_halves[core] + attn).astype(BF16)
+    share_half(nz, resid)
+    residual = jnp.concatenate([resid[0].astype(F32), resid[1].astype(F32)], axis=1)
     square_out = square_tile(jnp.sum(residual * residual, axis=1, keepdims=True)).reshape(nm, 8, HD)
-    normed = (residual * post_ref[...].astype(F32)).astype(BF16)
-    chunk = 256 if fh % 256 == 0 else 128
-    later_copies[3].wait()
-    later_copies[4].wait()
-    for c in range(2):
-
-        def up_step(i, _):
-            at = pl.multiple_of(c * fh + i * chunk, chunk)
-            gate = dot(normed, wg[:, pl.ds(at, chunk)]).reshape(nm, 8, chunk)
-            up = dot(normed, wu[:, pl.ds(at, chunk)]).reshape(nm, 8, chunk)
-            send4[:, c, :, pl.ds(pl.multiple_of(i * chunk, chunk), chunk)] = jnp.concatenate(
-                [gate, up], axis=1
+    square_out = jnp.concatenate([square_out, jnp.zeros_like(square_out)], axis=1).astype(BF16)
+    send_sq[:, 0] = square_out
+    send_sq[:, 1] = square_out
+    kvp_scatter(4, send_sq, recv_sq)
+    normed = (residual * post_ref[...].astype(F32).reshape(1, db)).astype(BF16)
+    arrive(3)
+    arrive(4)
+    for p, (at, size) in enumerate(pieces):
+        part = pl.ds(at, size)
+        started.append((kvp_copy, 5 + p, recv4.at[0, :, part], range(1, nk)))
+        for c in range(2):
+            columns = slice(c * fh + at, c * fh + at + size)
+            gate = dot(normed, wg[:, columns]).reshape(nm, 8, size)
+            up = dot(normed, wu[:, columns]).reshape(nm, 8, size)
+            send4[:, c, :, part] = jnp.concatenate([gate, up], axis=1).astype(BF16)
+
+            def step(i, _, p=p, c=c, part=part):
+                to_m = lax.rem(me_m + i, nm)
+                to = 2 * to_m + c
+                k = lax.rem(to - me_k + nk, nk)
+
+                @pl.when(k != 0)
+                def _():
+                    kvp_copy(5 + p, k, send4.at[to_m, c, :, part], recv4.at[me_k, :, part]).start()
+
+                return 0
+
+            lax.fori_loop(0, nm, step, 0)
+    total = kvp_reduce(4, send_sq, recv_sq)
+    inverse = lax.rsqrt(jnp.sum(total[:8], axis=1, keepdims=True) / width + EPSILON)
+    base = 5 + len(pieces)
+    for p, (at, size) in enumerate(pieces):
+        part = pl.ds(at, size)
+
+        def add(k, total, p=p, part=part):
+            source = lax.rem(me_k + k, nk)
+            kvp_wait(5 + p, source, recv4.at[source, :, part])
+            return total + recv4[source, :, part].astype(F32)
+
+        total = lax.fori_loop(1, nk, add, send4[me_m, me_c, :, part].astype(F32))
+        gate = total[:8] * inverse
+        up = total[8:] * inverse
+        middle = gate / (1.0 + jnp.exp(-gate)) * up
+        mine = gath4.at[me_m, me_c, :, pl.ds(at // 2, size // 2)]
+        mine[...] = folded(middle).astype(BF16)
+        started.append((kvp_copy, base + p, mine, range(1, nk)))
+
+        def share(k, _, p=p, mine=mine):
+            kvp_copy(base + p, k, mine, mine).start()
+            return 0
+
+        lax.fori_loop(1, nk, share, 0)
+    arrive(5)
+    down_part = jnp.zeros((rows, db), F32)
+    for p, (at, size) in enumerate(pieces):
+        part = pl.ds(at // 2, size // 2)
+
+        def await_hidden(k, _, p=p, part=part):
+            source = lax.rem(me_k + k, nk)
+            kvp_wait(base + p, source, gath4.at[source // 2, source % 2, :, part])
+            return 0
+
+        lax.fori_loop(1, nk, await_hidden, 0)
+        for c in range(2):
+            rows_of = [gath4[m, c, :, part].astype(F32) for m in range(nm)]
+            piece = jnp.concatenate(
+                [jnp.concatenate([r[:8] for r in rows_of], axis=0), jnp.concatenate([r[8:] for r in rows_of], axis=0)],
+                axis=1,
             ).astype(BF16)
-            return 0
-
-        lax.fori_loop(0, fh // chunk, up_step, 0)
-        send4[:, c, :, fh:] = jnp.concatenate([square_out, jnp.zeros_like(square_out)], axis=1).astype(BF16)
-        kvp_scatter(4, send4, recv4, only=c)
-    total = kvp_reduce(4, send4, recv4)
-    square_sum = jnp.sum(total[:8, fh:], axis=1, keepdims=True)
-    inverse = lax.rsqrt(square_sum / width + EPSILON)
-    gate = total[:8, :fh] * inverse
-    up = total[8:, :fh] * inverse
-    middle = gate / (1.0 + jnp.exp(-gate)) * up
-    gath4[me_m, me_c] = folded(middle).astype(BF16)
-    kvp_gather(5, gath4)
-    later_copies[5].wait()
-    kvp_gather_wait(5, gath4)
-    down_part = jnp.zeros((rows, db), F32)
-    for c in range(2):
-        for g in range(2):
-            piece = jnp.concatenate(
-                [gath4[m, c].astype(F32)[8 * g : 8 * g + 8] for m in range(nm)], axis=0
-            ).astype(BF16)
-            at = fh * c + fq * g
-            down_part += dot(piece, wd[at : at + fq, :])
-    down = head_sum(2, down_part, send5, recv5)
-    gath5[me_h] = (gath3[me_h].astype(F32) + down).astype(BF16)
-    head_gather(3, gath5)
-    next_ref[...] = unfolded(gath5).astype(BF16)
-
-    def kvp_done(k, _):
-        for phase, ref in ((0, recv1), (2, recv2), (4, recv4)):
-            kvp_copy(phase, k, ref.at[0], ref.at[0]).wait_send()
-        for phase, ref in ((1, gath1), (3, gath2), (5, gath4)):
-            kvp_copy(phase, k, ref.at[0, 0], ref.at[0, 0]).wait_send()
-        return 0
-
-    lax.fori_loop(1, nk, kvp_done, 0)
-
-    def head_done(k, _):
-        for phase, ref in ((0, recv3), (1, gath3), (2, recv5), (3, gath5)):
-            head_copy(phase, k, ref.at[0], ref.at[0]).wait_send()
-        return 0
-
-    lax.fori_loop(1, nh, head_done, 0)
+            down_part += dot(piece, wd[c * fh + at : c * fh + at + size, :])
+    down = head_sum(nz + 1, down_part, core5, along5)
+    final[core] = (resid[core].astype(F32) + down).astype(BF16)
+    share_half(2 * nz + 1, final)
+    next_ref[:, :half] = final[0]
+    next_ref[:, half:] = final[1]
+    finish()
 
 
 def body(
@@ -545,6 +584,7 @@
     nm = nk // 2
     slots = cache_keys.shape[0]
     fh = w_gate.shape[1] // 2
+    half, nz, count = db // 2, nh // 2, len(pieces_of(fh))
     exponent = np.arange(HD // 2, dtype=np.float32) * np.float32(2.0 / HD)
     frequency = (THETA_BASE ** (-exponent.astype(np.float64))).astype(np.float32)
     frequency = jnp.asarray(np.concatenate([frequency, frequency])[None, :])
@@ -556,7 +596,7 @@
         for w in (w_query, w_key, w_value, w_out, w_gate, w_up, w_down, cache_keys, cache_values)
     ]
     scratch += [
-        pltpu.VMEM((nh, 8, db), F32),
+        pltpu.VMEM((2, rows, half), F32),
         pltpu.VMEM((nm, 2, 16, 384), BF16),
         pltpu.VMEM((nk, 16, 384), BF16),
         pltpu.VMEM((nm, 2, 3, 16, HD), BF16),
@@ -570,23 +610,25 @@
         pltpu.VMEM((nm, 2, 48, HD), BF16),
         pltpu.VMEM((nk, 48, HD), BF16),
         pltpu.VMEM((nm, 2, 16, 256), BF16),
-        pltpu.VMEM((nh, 16, db // 2), BF16),
-        pltpu.VMEM((nh, 16, db // 2), BF16),
-        pltpu.VMEM((nh, 16, db // 2), BF16),
-        pltpu.VMEM((nm, 2, 16, fh + HD), BF16),
-        pltpu.VMEM((nk, 16, fh + HD), BF16),
+        pltpu.VMEM((2, rows, half), BF16),
+        pltpu.VMEM((nz, rows, half), BF16),
+        pltpu.VMEM((2, rows, half), BF16),
+        pltpu.VMEM((nm, 2, 16, HD), BF16),
+        pltpu.VMEM((nk, 16, HD), BF16),
+        pltpu.VMEM((nm, 2, 16, fh), BF16),
+        pltpu.VMEM((nk, 16, fh), BF16),
         pltpu.VMEM((nm, 2, 16, fh // 2), BF16),
-        pltpu.VMEM((nh, 16, db // 2), BF16),
-        pltpu.VMEM((nh, 16, db // 2), BF16),
-        pltpu.VMEM((nh, 16, db // 2), BF16),
+        pltpu.VMEM((2, rows, half), BF16),
+        pltpu.VMEM((nz, rows, half), BF16),
+        pltpu.VMEM((2, rows, half), BF16),
         pltpu.SemaphoreType.DMA((9,)),
-        pltpu.SemaphoreType.DMA((6, nk)),
-        pltpu.SemaphoreType.DMA((6, nk)),
-        pltpu.SemaphoreType.DMA((4, nh)),
-        pltpu.SemaphoreType.DMA((4, nh)),
+        pltpu.SemaphoreType.DMA((5 + 2 * count, nk)),
+        pltpu.SemaphoreType.DMA((5 + 2 * count, nk)),
+        pltpu.SemaphoreType.DMA((2 * nz + 2,)),
+        pltpu.SemaphoreType.DMA((2 * nz + 2,)),
     ]
     weight_items = sum(w.size for w in (w_query, w_key, w_value, w_out, w_gate, w_up, w_down))
-    return pl.pallas_call(
+    results = pl.pallas_call(
         functools.partial(kernel, nk, nh, db * nk),
         out_shape=(
             jax.ShapeDtypeStruct((rows, db), BF16),
@@ -606,8 +648,8 @@
         ),
     )(
         hidden_in,
-        norm_gain.reshape(1, db),
-        post_gain.reshape(1, db),
+        norm_gain,
+        post_gain,
         frequency,
         w_query,
         w_key,
@@ -622,6 +664,13 @@
         slot_request,
         slot_start,
     )
+    return pl.pallas_call(
+        hand_on,
+        out_shape=tuple(jax.ShapeDtypeStruct(r.shape, r.dtype) for r in results),
+        in_specs=[hbm] * 3,
+        out_specs=(hbm,) * 3,
+        scratch_shapes=[pltpu.SemaphoreType.DMA((3,))],
+    )(*results)
 
 
 def solution(mesh):

time: 91.5 us -> 79.8 us (0.87)
  local copies, waits for them, and re-layouts: 6.64 us -> 0 us
  Pallas kernels: 83.9 us -> 79 us
    pallas_call x1, Pallas kernels: 83.9 us -> 74.9 us  [body(): pl.pallas_call(functools.partial(kernel, nk, nh, db * nk), out_shape=(jax...]
    unnamed x3 -> x0, local copies, waits for them, and re-layouts: 4.12 us -> none
    pallas_call x0 -> x1, Pallas kernels: none -> 4.11 us  [body(): pl.pallas_call(hand_on, out_shape=tuple((jax.ShapeDtypeStruct(r.shape, r....]
    reshape x2 -> x0, local copies, waits for them, and re-layouts: 2.52 us -> none  [the longest x1 1.26 us: body(): norm_gain.reshape(1, db)]
where the time goes in v2:
time: 79.8 us; the launch traced here: 79.7 us
  Pallas kernels  79 us (99%)
    pallas_call x1, Pallas kernels, body(): pl.pallas_call(functools.partial(kernel, nk, nh, db * nk), out_shape=(jax...  74.9 us
    pallas_call x1, Pallas kernels, body(): pl.pallas_call(hand_on, out_shape=tuple((jax.ShapeDtypeStruct(r.shape, r....  4.11 us

profile of v2, /device:TPU:1, one launch (start us, length us, event | category | flops | bytes accessed | tf_op | source)
XLA Modules:
  0.0 79.7 jit_solution(7199502614190677722)
XLA Ops:
  0.6 74.9 %shard_map.175 = (bf16[64,512]{1,0:T(8,128)(2,1)}, bf16[64,128]{1,0:T(8,128)(2,1)}, bf16[64,128]{1,0:T(8,128)(2,1)}) custom-call(bf16[64,512]{1,0:T(8,128)(2,1)} %hid_ref.1, bf16[512]{0:T(512)(128)(2,1)} %gain_ref.1, bf16[512]{0:T(512)(128)(2,1)} %post_ref.1, f32[1,128]{1,0:T(1,128)} %constant.2.clone.freq_ref, bf16[512,1024]{1,0:T(8,128)(2,1)} %wq_hbm.1, ...), custom_call_target="tpu_custom_call" | custom-call | flops 1191182336 | bytes 23855104 | tf_op jit(solution)/shard_map/pallas_call | solution.py:631
  75.5 4.1 %shard_map.176 = (bf16[64,512]{1,0:T(8,128)(2,1)}, bf16[64,128]{1,0:T(8,128)(2,1)}, bf16[64,128]{1,0:T(8,128)(2,1)}) custom-call(bf16[64,512]{1,0:T(8,128)(2,1)} %get-tuple-element.6.refs_0_, bf16[64,128]{1,0:T(8,128)(2,1)} %get-tuple-element.7.refs_1_, bf16[64,128]{1,0:T(8,128)(2,1)} %get-tuple-element.8.refs_2_), custom_call_target="tpu_custom_call" | custom-call | tf_op jit(solution)/shard_map/pallas_call | solution.py:667

commit v3 on v2

--- a/solution.py
+++ b/solution.py
@@ -42,17 +42,15 @@
 
 
 def pieces_of(columns):
-    size = 512 if columns > 512 else columns // 2
-    return [(at, min(size, columns - at)) for at in range(0, columns, size)]
-
-
-def hand_on(*refs):
-    sources, targets, sem = refs[:3], refs[3:6], refs[6]
-    copies = [pltpu.make_async_copy(a, b, sem.at[i]) for i, (a, b) in enumerate(zip(sources, targets))]
-    for copy in copies:
-        copy.start()
-    for copy in copies:
-        copy.wait()
+    size = 512 if columns > 1024 else 256
+    starts = range(0, columns, size)
+    return [(at, min(size, columns - at), "xy"[i] if i < 2 else None) for i, at in enumerate(starts)]
+
+
+def hand_on(a_ref, b_ref, c_ref, a_out, b_out, c_out):
+    a_out[...] = a_ref[...]
+    b_out[...] = b_ref[...]
+    c_out[...] = c_ref[...]
 
 
 def kernel(
@@ -91,13 +89,12 @@
     send1,
     recv1,
     gath1,
-    queries,
+    draft_kv,
     scores,
     runs,
     tops,
     outs,
     sums,
-    lasts,
     send2,
     recv2,
     gath2,
@@ -108,6 +105,10 @@
     recv_sq,
     send4,
     recv4,
+    line_recv_x,
+    line_recv,
+    line_sum,
+    cross_recv,
     gath4,
     core5,
     along5,
@@ -117,6 +118,8 @@
     krecv_sem,
     hsend_sem,
     hrecv_sem,
+    lsend_sem,
+    lrecv_sem,
 ):
     me_k = lax.axis_index("kvp")
     me_h = lax.axis_index("head")
@@ -130,6 +133,8 @@
 
     rows = 8 * nm
     me_m, me_c = me_k // 2, me_k % 2
+    side = math.isqrt(nk)
+    me_y, me_x = me_k // side, me_k % side
     slots = keys.shape[0]
     db = hid_ref.shape[1]
     half = db // 2
@@ -137,7 +142,6 @@
     fh = ff // 2
     pieces = pieces_of(fh)
 
-    started = []
     sent = []
 
     first_copies = [
@@ -158,34 +162,35 @@
 
     barrier = pltpu.get_barrier_semaphore()
 
-    def greet_k(k, _):
-        pl.semaphore_signal(barrier, inc=1, device_id=(lax.rem(me_k + k, nk), me_h), device_id_type=MESH)
-        return 0
-
-    lax.fori_loop(1, nk, greet_k, 0)
+    offsets = [(dy, dx) for dy in range(side) for dx in range(side) if dy or dx]
+    offsets.sort(key=lambda o: -sum(min(d, side - d) for d in o))
+    targets = [
+        lax.rem(me_y + dy, side) * side + lax.rem(me_x + dx, side) for dy, dx in offsets
+    ]
+    sources = [
+        lax.rem(me_y + side - dy, side) * side + lax.rem(me_x + side - dx, side) for dy, dx in offsets
+    ]
+    near_first = list(reversed(range(nk - 1)))
+
+    for to in targets:
+        pl.semaphore_signal(barrier, inc=1, device_id=(to, me_h), device_id_type=MESH)
     for to in [twin] + [along_z(k) for k in range(1, nz)]:
         pl.semaphore_signal(barrier, inc=1, device_id=(me_k, to), device_id_type=MESH)
 
-    def kvp_copy(phase, k, src, dst):
-        to = lax.rem(me_k + k, nk)
+    def kvp_copy(phase, i, src, dst):
         return pltpu.make_async_remote_copy(
             src_ref=src,
             dst_ref=dst,
-            send_sem=ksend_sem.at[phase, k],
-            recv_sem=krecv_sem.at[phase, me_k],
-            device_id=(to, me_h),
+            send_sem=ksend_sem.at[phase, i],
+            recv_sem=krecv_sem.at[phase, i],
+            device_id=(targets[i], me_h),
             device_id_type=MESH,
         )
 
-    def kvp_wait(phase, source, ref):
-        pltpu.make_async_remote_copy(
-            src_ref=ref,
-            dst_ref=ref,
-            send_sem=ksend_sem.at[phase, 0],
-            recv_sem=krecv_sem.at[phase, source],
-            device_id=(source, me_h),
-            device_id_type=MESH,
-        ).wait_recv()
+    def kvp_start(phase, i, src, dst):
+        copy = kvp_copy(phase, i, src, dst)
+        copy.start()
+        sent.append(copy)
 
     def head_copy(sem, to, src, dst):
         return pltpu.make_async_remote_copy(
@@ -197,41 +202,44 @@
             device_id_type=MESH,
         )
 
+    def line_copy(sem, k, axis, src, dst):
+        if axis == "x":
+            to = me_y * side + lax.rem(me_x + k, side)
+        else:
+            to = lax.rem(me_y + k, side) * side + me_x
+        copy = pltpu.make_async_remote_copy(
+            src_ref=src,
+            dst_ref=dst,
+            send_sem=lsend_sem.at[sem, k],
+            recv_sem=lrecv_sem.at[sem, k],
+            device_id=(to, me_h),
+            device_id_type=MESH,
+        )
+        copy.start()
+        sent.append(copy)
+        return copy
+
     def kvp_scatter(phase, send, recv):
-        started.append((kvp_copy, phase, recv.at[0], range(1, nk)))
-
-        def step(k, _):
-            to = lax.rem(me_k + k, nk)
-            kvp_copy(phase, k, send.at[to // 2, to % 2], recv.at[me_k]).start()
-            return 0
-
-        lax.fori_loop(1, nk, step, 0)
-
-    def kvp_gather(phase, gath):
-        mine = gath.at[me_m, me_c]
-        started.append((kvp_copy, phase, mine, range(1, nk)))
-
-        def step(k, _):
-            kvp_copy(phase, k, mine, mine).start()
-            return 0
-
-        lax.fori_loop(1, nk, step, 0)
-
-    def kvp_gather_wait(phase, gath):
-        def step(k, _):
-            source = lax.rem(me_k + k, nk)
-            kvp_wait(phase, source, gath.at[source // 2, source % 2])
-            return 0
-
-        lax.fori_loop(1, nk, step, 0)
-
-    def kvp_reduce(phase, send, recv):
-        def step(k, total):
-            source = lax.rem(me_k + k, nk)
-            kvp_wait(phase, source, recv.at[source])
-            return total + recv[source].astype(F32)
-
-        return lax.fori_loop(1, nk, step, send[me_m, me_c].astype(F32))
+        for i, to in enumerate(targets):
+            kvp_start(phase, i, send.at[to // 2, to % 2], recv.at[i])
+
+    def kvp_gather(phase, mine):
+        for i in range(nk - 1):
+            kvp_start(phase, i, mine, mine)
+
+    def kvp_await(phase, i, ref):
+        kvp_copy(phase, i, ref, ref).wait_recv()
+
+    def kvp_gather_wait(phase, slot):
+        for i in near_first:
+            kvp_await(phase, i, slot(sources[i]))
+
+    def kvp_reduce(phase, own, recv):
+        total = own.astype(F32)
+        for i in near_first:
+            kvp_await(phase, i, recv.at[i])
+            total = total + recv[i].astype(F32)
+        return total
 
     def halves(x):
         return x[:, :half], x[:, half:]
@@ -266,15 +274,8 @@
         copy.wait_recv()
 
     def finish():
-        for copy in sent:
-            copy.wait_send()
-        for copy, phase, ref, keys_of in started:
-
-            def done(k, _, copy=copy, phase=phase, ref=ref):
-                copy(phase, k, ref, ref).wait_send()
-                return 0
-
-            lax.fori_loop(keys_of.start, keys_of.stop, done, 0)
+        while sent:
+            sent.pop(0).wait_send()
 
     def folded(x):
         return jnp.concatenate([x[:, : x.shape[1] // 2], x[:, x.shape[1] // 2 :]], axis=0)
@@ -302,9 +303,6 @@
         lower = jnp.concatenate([query_part[:, 384:], value_part if c else key_part, square_in], axis=1)
         send1[:, c] = jnp.concatenate([upper.reshape(nm, 8, 384), lower.reshape(nm, 8, 384)], axis=1).astype(BF16)
 
-    pl.semaphore_wait(barrier, nk + nz - 1)
-    kvp_scatter(0, send1, recv1)
-
     eight = iota((8, HD), 0)
     lane8 = iota((8, HD), 1)
     position = jnp.where(eight < DRAFT, ctx_ref[2 * me_m], ctx_ref[2 * me_m + 1]) + eight % DRAFT
@@ -316,9 +314,12 @@
     def find_last(s, last):
         return jnp.where(lane8 == req_ref[s], s, last)
 
-    lasts[...] = lax.fori_loop(0, slots, find_last, jnp.full((8, HD), -1, jnp.int32), unroll=8)
-
-    total = kvp_reduce(0, send1, recv1)
+    last_slots = lax.fori_loop(0, slots, find_last, jnp.full((8, HD), -1, jnp.int32), unroll=8)
+    last_of = [jnp.max(jnp.where(lane8 == b, last_slots, -1)) for b in range(nk)]
+    pl.semaphore_wait(barrier, nk + nz - 1)
+    kvp_scatter(0, send1, recv1)
+
+    total = kvp_reduce(0, send1[me_m, me_c], recv1)
     square_sum = jnp.sum(total[8:, 256:], axis=1, keepdims=True)
     inverse = lax.rsqrt(square_sum / width + EPSILON)
     tiles = [total[:8, :128], total[:8, 128:256], total[:8, 256:], total[8:, :128], total[8:, 128:256]]
@@ -337,21 +338,14 @@
 
     q0, q1, q2, q3 = rotated[:4]
     pair = jnp.where(me_c == 0, rotated[4], tiles[4])
-    gath1[me_m, me_c, 0] = jnp.concatenate([first_of(q0, q1), first_of(q2, q3)], axis=0).astype(BF16)
-    gath1[me_m, me_c, 1] = jnp.concatenate([second_of(q0, q1), second_of(q2, q3)], axis=0).astype(BF16)
-    gath1[me_m, me_c, 2] = jnp.concatenate([pair, jnp.zeros_like(pair)], axis=0).astype(BF16)
-    kvp_gather(1, gath1)
-    kvp_gather_wait(1, gath1)
-    for m in range(nm):
-        for s in range(2):
-            queries[2 * m + s, :16] = gath1[m, 0, s]
-            queries[2 * m + s, 16:] = gath1[m, 1, s]
-    drafts = [
-        jnp.concatenate([gath1[m, c, 2].astype(F32)[:8] for m in range(nm)], axis=0).astype(BF16) for c in range(2)
-    ]
-    dkey_ref[...] = drafts[0]
-    dval_ref[...] = drafts[1]
-
+    query_slot = gath1.at[pl.ds(2 * me_m, 2), me_c]
+    query_slot[0] = jnp.concatenate([first_of(q0, q1), first_of(q2, q3)], axis=0).astype(BF16)
+    query_slot[1] = jnp.concatenate([second_of(q0, q1), second_of(q2, q3)], axis=0).astype(BF16)
+    draft_kv[me_m, me_c] = jnp.concatenate([pair, jnp.zeros_like(pair)], axis=0).astype(BF16)
+    kvp_gather(1, query_slot)
+    kv_phase = 5 + 2 * len(pieces)
+    kvp_gather(kv_phase, draft_kv.at[me_m, me_c])
+    kvp_gather_wait(1, lambda source: gath1.at[pl.ds(2 * (source // 2), 2), source % 2])
     arrive(0)
     token = iota((32, BLOCK), 1)
 
@@ -364,7 +358,7 @@
             r = req_ref[s]
             safe = jnp.maximum(r, 0)
             live = jnp.where(r >= 0, ctx_ref[safe] - start_ref[s], 0)
-            part = jnp.where(token < live, dot_t(queries[safe], keys[s]), FLOOR)
+            part = jnp.where(token < live, dot_t(gath1[safe].reshape(32, HD), keys[s]), FLOOR)
             scores[s] = part
             run = jnp.maximum(part, jnp.where(r == previous(s), run, FLOOR))
             runs[s] = run
@@ -372,7 +366,6 @@
 
     floor_tile = jnp.full((32, BLOCK), FLOOR, F32)
     lax.fori_loop(0, slots // UNROLL, score_step, floor_tile)
-    last_of = [jnp.max(jnp.where(lane8 == b, lasts[...], -1)) for b in range(nk)]
     for b in range(nk):
         run = runs[jnp.maximum(last_of[b], 0)]
         top = jnp.max(run, axis=1, keepdims=True)
@@ -428,25 +421,24 @@
             send2[m, c, 32:48, :] = tile.astype(BF16)
     kvp_scatter(2, send2, recv2)
 
-    mine = jnp.concatenate([gath1[me_m, me_c, 0], gath1[me_m, me_c, 1]], axis=0)
-    draft_score = dot_t(mine, gath1[me_m, 0, 2])
+    finish()
+    kvp_gather_wait(kv_phase, lambda source: draft_kv.at[source // 2, source % 2])
+    for c, out_ref in enumerate((dkey_ref, dval_ref)):
+        out_ref[...] = jnp.concatenate([draft_kv[m, c].astype(F32)[:8] for m in range(nm)], axis=0).astype(BF16)
+    mine = gath1[pl.ds(2 * me_m, 2), me_c].reshape(32, HD)
+    draft_score = dot_t(mine, draft_kv[me_m, 0])
     row16, col16 = iota((32, 16), 0), iota((32, 16), 1)
     seen = (col16 // DRAFT == row16 // 16) & (col16 % DRAFT <= row16 % DRAFT)
     draft_score = jnp.where(seen, draft_score, FLOOR)
     draft_top = jnp.max(draft_score, axis=1, keepdims=True)
     draft_weight = jnp.where(seen, jnp.exp2((draft_score - draft_top) * EXP_SCALE), 0.0)
     draft_sum = jnp.sum(draft_weight, axis=1, keepdims=True)
-    draft_out = dot(draft_weight.astype(BF16), gath1[me_m, 1, 2])
-
-    recv2[me_k] = send2[me_m, me_c]
-
-    def wait2(k, _):
-        source = lax.rem(me_k + k, nk)
-        kvp_wait(2, source, recv2.at[source])
-        return 0
-
-    lax.fori_loop(1, nk, wait2, 0)
-    every = [recv2[i, 32:48, :].astype(F32)[:8] for i in range(nk)]
+    draft_out = dot(draft_weight.astype(BF16), draft_kv[me_m, 1])
+
+    for i in near_first:
+        kvp_await(2, i, recv2.at[i])
+    partials = [send2.at[me_m, me_c]] + [recv2.at[i] for i in range(nk - 1)]
+    every = [p[32:48, :].astype(F32)[:8] for p in partials]
     every = jnp.concatenate(every + [jnp.zeros((8, HD), F32)] * (HD // 8 - nk), axis=0)
     turned = every.T[:32]
     joined = turned + pltpu.roll(turned, HD - 1, 1) + pltpu.roll(turned, HD - 2, 1)
@@ -460,16 +452,17 @@
     factor = factor / whole
     mixed = draft_out * (draft_factor / whole)
     for i in range(nk):
-        mixed = mixed + recv2[i, :32, :].astype(F32) * factor[:, 8 * i : 8 * i + 1]
+        mixed = mixed + partials[i][:32, :].astype(F32) * factor[:, 8 * i : 8 * i + 1]
     a0, a1, b0, b1 = mixed[:8], mixed[8:16], mixed[16:24], mixed[24:]
     h0, h1 = first_of(a0, b0), second_of(a0, b0)
     h2, h3 = first_of(a1, b1), second_of(a1, b1)
     gath2[me_m, me_c] = jnp.concatenate(
         [jnp.concatenate([h0, h1], axis=1), jnp.concatenate([h2, h3], axis=1)], axis=0
     ).astype(BF16)
-    kvp_gather(3, gath2)
+    kvp_gather(3, gath2.at[me_m, me_c])
+    finish()
     arrive(2)
-    kvp_gather_wait(3, gath2)
+    kvp_gather_wait(3, lambda source: gath2.at[source // 2, source % 2])
 
     attn_part = jnp.zeros((rows, db), F32)
     for c in range(2):
@@ -482,70 +475,95 @@
     resid[core] = (hidden_halves[core] + attn).astype(BF16)
     share_half(nz, resid)
     residual = jnp.concatenate([resid[0].astype(F32), resid[1].astype(F32)], axis=1)
-    square_out = square_tile(jnp.sum(residual * residual, axis=1, keepdims=True)).reshape(nm, 8, HD)
-    square_out = jnp.concatenate([square_out, jnp.zeros_like(square_out)], axis=1).astype(BF16)
-    send_sq[:, 0] = square_out
-    send_sq[:, 1] = square_out
-    kvp_scatter(4, send_sq, recv_sq)
     normed = (residual * post_ref[...].astype(F32).reshape(1, db)).astype(BF16)
     arrive(3)
     arrive(4)
-    for p, (at, size) in enumerate(pieces):
+    lines, direct = {}, []
+    for p, (at, size, axis) in enumerate(pieces):
         part = pl.ds(at, size)
-        started.append((kvp_copy, 5 + p, recv4.at[0, :, part], range(1, nk)))
         for c in range(2):
             columns = slice(c * fh + at, c * fh + at + size)
             gate = dot(normed, wg[:, columns]).reshape(nm, 8, size)
             up = dot(normed, wu[:, columns]).reshape(nm, 8, size)
-            send4[:, c, :, part] = jnp.concatenate([gate, up], axis=1).astype(BF16)
-
-            def step(i, _, p=p, c=c, part=part):
-                to_m = lax.rem(me_m + i, nm)
-                to = 2 * to_m + c
-                k = lax.rem(to - me_k + nk, nk)
-
-                @pl.when(k != 0)
-                def _():
-                    kvp_copy(5 + p, k, send4.at[to_m, c, :, part], recv4.at[me_k, :, part]).start()
-
-                return 0
-
-            lax.fori_loop(0, nm, step, 0)
-    total = kvp_reduce(4, send_sq, recv_sq)
+            both = jnp.concatenate([gate, up], axis=1).astype(BF16)
+            send4[:, :, c, :, part] = both.reshape(side, side // 2, 16, size)
+        if axis is None:
+            direct.append((p, part))
+            continue
+        lines[p] = []
+        for k in [side // 2] + [k for k in range(1, side) if k != side // 2]:
+            if axis == "x":
+                x = lax.rem(me_x + k, side)
+                src, dst = send4.at[:, x // 2, x % 2, :, part], line_recv_x.at[k - 1, :, :, part]
+            else:
+                y = lax.rem(me_y + k, side)
+                src, dst = send4.at[y, :, :, :, part], line_recv.at[k - 1, :, :, :, part]
+            lines[p].append(line_copy(p, k, axis, src, dst))
+        if p == 0:
+            square_out = square_tile(jnp.sum(residual * residual, axis=1, keepdims=True)).reshape(nm, 8, HD)
+            square_out = jnp.concatenate([square_out, jnp.zeros_like(square_out)], axis=1).astype(BF16)
+            send_sq[:, 0] = square_out
+            send_sq[:, 1] = square_out
+            kvp_scatter(4, send_sq, recv_sq)
+    finish()
+    for p, part in direct:
+        for i, to in enumerate(targets):
+            src = send4.at[to // side, (to % side) // 2, to % 2, :, part]
+            kvp_start(5 + p, i, src, recv4.at[i, :, part])
+    crossing = {}
+    for p, (at, size, axis) in enumerate(pieces):
+        if axis is None:
+            continue
+        part = pl.ds(at, size)
+        for copy in lines[p]:
+            copy.wait_recv()
+        if axis == "x":
+            own, here = send4[:, me_x // 2, me_x % 2, :, part], me_y
+        else:
+            own, here = send4[me_y, :, :, :, part].reshape(side, 16, size), me_x
+        total = own.astype(F32)
+        for k in range(1, side):
+            if axis == "x":
+                total = total + line_recv_x[k - 1, :, :, part].astype(F32)
+            else:
+                total = total + line_recv[k - 1, :, :, :, part].astype(F32).reshape(side, 16, size)
+        line_sum[:, :, part] = total.astype(BF16)
+        crossing[p] = [
+            line_copy(
+                2 + p,
+                k,
+                "y" if axis == "x" else "x",
+                line_sum.at[lax.rem(here + k, side), :, part],
+                cross_recv.at[k - 1, :, part],
+            )
+            for k in range(1, side)
+        ]
+    total = kvp_reduce(4, send_sq[me_m, me_c], recv_sq)
     inverse = lax.rsqrt(jnp.sum(total[:8], axis=1, keepdims=True) / width + EPSILON)
     base = 5 + len(pieces)
-    for p, (at, size) in enumerate(pieces):
+    for p, (at, size, axis) in enumerate(pieces):
         part = pl.ds(at, size)
-
-        def add(k, total, p=p, part=part):
-            source = lax.rem(me_k + k, nk)
-            kvp_wait(5 + p, source, recv4.at[source, :, part])
-            return total + recv4[source, :, part].astype(F32)
-
-        total = lax.fori_loop(1, nk, add, send4[me_m, me_c, :, part].astype(F32))
+        if axis is None:
+            own = send4[me_y, me_x // 2, me_c, :, part]
+            total = kvp_reduce(5 + p, own, recv4.at[:, :, part])
+        else:
+            for copy in crossing[p]:
+                copy.wait_recv()
+            total = line_sum[me_y if axis == "x" else me_x, :, part].astype(F32)
+            for k in range(1, side):
+                total = total + cross_recv[k - 1, :, part].astype(F32)
         gate = total[:8] * inverse
         up = total[8:] * inverse
         middle = gate / (1.0 + jnp.exp(-gate)) * up
         mine = gath4.at[me_m, me_c, :, pl.ds(at // 2, size // 2)]
         mine[...] = folded(middle).astype(BF16)
-        started.append((kvp_copy, base + p, mine, range(1, nk)))
-
-        def share(k, _, p=p, mine=mine):
-            kvp_copy(base + p, k, mine, mine).start()
-            return 0
-
-        lax.fori_loop(1, nk, share, 0)
+        kvp_gather(base + p, mine)
+    finish()
     arrive(5)
     down_part = jnp.zeros((rows, db), F32)
-    for p, (at, size) in enumerate(pieces):
+    for p, (at, size, _) in enumerate(pieces):
         part = pl.ds(at // 2, size // 2)
-
-        def await_hidden(k, _, p=p, part=part):
-            source = lax.rem(me_k + k, nk)
-            kvp_wait(base + p, source, gath4.at[source // 2, source % 2, :, part])
-            return 0
-
-        lax.fori_loop(1, nk, await_hidden, 0)
+        kvp_gather_wait(base + p, lambda source, part=part: gath4.at[source // 2, source % 2, :, part])
         for c in range(2):
             rows_of = [gath4[m, c, :, part].astype(F32) for m in range(nm)]
             piece = jnp.concatenate(
@@ -584,7 +602,7 @@
     nm = nk // 2
     slots = cache_keys.shape[0]
     fh = w_gate.shape[1] // 2
-    half, nz, count = db // 2, nh // 2, len(pieces_of(fh))
+    half, nz, side, count = db // 2, nh // 2, math.isqrt(nk), len(pieces_of(fh))
     exponent = np.arange(HD // 2, dtype=np.float32) * np.float32(2.0 / HD)
     frequency = (THETA_BASE ** (-exponent.astype(np.float64))).astype(np.float32)
     frequency = jnp.asarray(np.concatenate([frequency, frequency])[None, :])
@@ -598,34 +616,39 @@
     scratch += [
         pltpu.VMEM((2, rows, half), F32),
         pltpu.VMEM((nm, 2, 16, 384), BF16),
-        pltpu.VMEM((nk, 16, 384), BF16),
-        pltpu.VMEM((nm, 2, 3, 16, HD), BF16),
-        pltpu.VMEM((nk, 32, HD), BF16),
+        pltpu.VMEM((nk - 1, 16, 384), BF16),
+        pltpu.VMEM((nk, 2, 16, HD), BF16),
+        pltpu.VMEM((nm, 2, 16, HD), BF16),
         pltpu.VMEM((slots, 32, BLOCK), F32),
         pltpu.VMEM((slots, 32, BLOCK), F32),
         pltpu.VMEM((nk, 32, BLOCK), F32),
         pltpu.VMEM((slots, 32, HD), F32),
         pltpu.VMEM((slots, 32, BLOCK), F32),
-        pltpu.VMEM((8, HD), jnp.int32),
         pltpu.VMEM((nm, 2, 48, HD), BF16),
-        pltpu.VMEM((nk, 48, HD), BF16),
+        pltpu.VMEM((nk - 1, 48, HD), BF16),
         pltpu.VMEM((nm, 2, 16, 256), BF16),
         pltpu.VMEM((2, rows, half), BF16),
         pltpu.VMEM((nz, rows, half), BF16),
         pltpu.VMEM((2, rows, half), BF16),
         pltpu.VMEM((nm, 2, 16, HD), BF16),
-        pltpu.VMEM((nk, 16, HD), BF16),
-        pltpu.VMEM((nm, 2, 16, fh), BF16),
-        pltpu.VMEM((nk, 16, fh), BF16),
+        pltpu.VMEM((nk - 1, 16, HD), BF16),
+        pltpu.VMEM((side, side // 2, 2, 16, fh), BF16),
+        pltpu.VMEM((nk - 1, 16, fh), BF16),
+        pltpu.VMEM((side - 1, side, 16, fh), BF16),
+        pltpu.VMEM((side - 1, side // 2, 2, 16, fh), BF16),
+        pltpu.VMEM((side, 16, fh), BF16),
+        pltpu.VMEM((side - 1, 16, fh), BF16),
         pltpu.VMEM((nm, 2, 16, fh // 2), BF16),
         pltpu.VMEM((2, rows, half), BF16),
         pltpu.VMEM((nz, rows, half), BF16),
         pltpu.VMEM((2, rows, half), BF16),
         pltpu.SemaphoreType.DMA((9,)),
-        pltpu.SemaphoreType.DMA((5 + 2 * count, nk)),
-        pltpu.SemaphoreType.DMA((5 + 2 * count, nk)),
+        pltpu.SemaphoreType.DMA((6 + 2 * count, nk)),
+        pltpu.SemaphoreType.DMA((6 + 2 * count, nk)),
         pltpu.SemaphoreType.DMA((2 * nz + 2,)),
         pltpu.SemaphoreType.DMA((2 * nz + 2,)),
+        pltpu.SemaphoreType.DMA((4, side)),
+        pltpu.SemaphoreType.DMA((4, side)),
     ]
     weight_items = sum(w.size for w in (w_query, w_key, w_value, w_out, w_gate, w_up, w_down))
     results = pl.pallas_call(
@@ -667,9 +690,8 @@
     return pl.pallas_call(
         hand_on,
         out_shape=tuple(jax.ShapeDtypeStruct(r.shape, r.dtype) for r in results),
-        in_specs=[hbm] * 3,
-        out_specs=(hbm,) * 3,
-        scratch_shapes=[pltpu.SemaphoreType.DMA((3,))],
+        in_specs=[vmem] * 3,
+        out_specs=(vmem,) * 3,
     )(*results)
 
 

time: 79.8 us -> 74.3 us (0.931)
  Pallas kernels: 79 us -> 73.4 us
    pallas_call x1, Pallas kernels: 74.9 us -> 71.9 us  [body(): pl.pallas_call(functools.partial(kernel, nk, nh, db * nk), out_shape=(jax...]
    pallas_call x1, Pallas kernels: 4.11 us -> 1.5 us  [body(): pl.pallas_call(hand_on, out_shape=tuple((jax.ShapeDtypeStruct(r.shape, r....]
where the time goes in v3:
time: 74.3 us; the launch traced here: 74.1 us
  Pallas kernels  73.4 us (99%)
    pallas_call x1, Pallas kernels, body(): pl.pallas_call(functools.partial(kernel, nk, nh, db * nk), out_shape=(jax...  71.9 us
    pallas_call x1, Pallas kernels, body(): pl.pallas_call(hand_on, out_shape=tuple((jax.ShapeDtypeStruct(r.shape, r....  1.5 us

profile of v3, /device:TPU:1, one launch (start us, length us, event | category | flops | bytes accessed | tf_op | source)
XLA Modules:
  0.0 74.1 jit_solution(13860192409022570666)
XLA Ops:
  0.6 71.9 %shard_map.175 = (bf16[64,512]{1,0:T(8,128)(2,1)}, bf16[64,128]{1,0:T(8,128)(2,1)}, bf16[64,128]{1,0:T(8,128)(2,1)}) custom-call(bf16[64,512]{1,0:T(8,128)(2,1)} %hid_ref.1, bf16[512]{0:T(512)(128)(2,1)} %gain_ref.1, bf16[512]{0:T(512)(128)(2,1)} %post_ref.1, f32[1,128]{1,0:T(1,128)} %constant.2.clone.freq_ref, bf16[512,1024]{1,0:T(8,128)(2,1)} %wq_hbm.1, ...), custom_call_target="tpu_custom_call" | custom-call | flops 1191182336 | bytes 23855104 | tf_op jit(solution)/shard_map/pallas_call | solution.py:654
  72.6 1.5 %shard_map.176 = (bf16[64,512]{1,0:T(8,128)(2,1)}, bf16[64,128]{1,0:T(8,128)(2,1)}, bf16[64,128]{1,0:T(8,128)(2,1)}) custom-call(bf16[64,512]{1,0:T(8,128)(2,1)} %get-tuple-element.6.a_ref, bf16[64,128]{1,0:T(8,128)(2,1)} %get-tuple-element.7.b_ref, bf16[64,128]{1,0:T(8,128)(2,1)} %get-tuple-element.8.c_ref), custom_call_target="tpu_custom_call" | custom-call | tf_op jit(solution)/shard_map/pallas_call | solution.py:690

commit v4 on v3

--- a/solution.py
+++ b/solution.py
@@ -17,7 +17,7 @@
 FLOOR = -1e30
 LOG2E = math.log2(math.e)
 EXP_SCALE = LOG2E / math.sqrt(HD)
-UNROLL = 32
+UNROLL = 80
 MESH = pl.DeviceIdType.MESH
 F32 = jnp.float32
 BF16 = jnp.bfloat16
@@ -42,9 +42,8 @@
 
 
 def pieces_of(columns):
-    size = 512 if columns > 1024 else 256
-    starts = range(0, columns, size)
-    return [(at, min(size, columns - at), "xy"[i] if i < 2 else None) for i, at in enumerate(starts)]
+    size = max(256, columns * 3 // 7 // 256 * 256)
+    return [(0, size, "x"), (size, size, "y"), (2 * size, columns - 2 * size, None)]
 
 
 def hand_on(a_ref, b_ref, c_ref, a_out, b_out, c_out):
@@ -90,6 +89,7 @@
     recv1,
     gath1,
     draft_kv,
+    turned_keys,
     scores,
     runs,
     tops,
@@ -319,6 +319,16 @@
     pl.semaphore_wait(barrier, nk + nz - 1)
     kvp_scatter(0, send1, recv1)
 
+    arrive(0)
+
+    def turn_keys(i, _):
+        for u in range(4):
+            n = 4 * i + u
+            turned_keys[n, :, :BLOCK] = keys[2 * n].T
+            turned_keys[n, :, BLOCK:] = keys[2 * n + 1].T
+        return 0
+
+    lax.fori_loop(0, slots // 8, turn_keys, 0)
     total = kvp_reduce(0, send1[me_m, me_c], recv1)
     square_sum = jnp.sum(total[8:, 256:], axis=1, keepdims=True)
     inverse = lax.rsqrt(square_sum / width + EPSILON)
@@ -346,22 +356,26 @@
     kv_phase = 5 + 2 * len(pieces)
     kvp_gather(kv_phase, draft_kv.at[me_m, me_c])
     kvp_gather_wait(1, lambda source: gath1.at[pl.ds(2 * (source // 2), 2), source % 2])
-    arrive(0)
     token = iota((32, BLOCK), 1)
 
     def previous(s):
         return req_ref[jnp.maximum(s - 1, 0)]
 
     def score_step(i, run):
-        for u in range(UNROLL):
+        for u in range(0, UNROLL, 2):
             s = i * UNROLL + u
-            r = req_ref[s]
-            safe = jnp.maximum(r, 0)
-            live = jnp.where(r >= 0, ctx_ref[safe] - start_ref[s], 0)
-            part = jnp.where(token < live, dot_t(gath1[safe].reshape(32, HD), keys[s]), FLOOR)
-            scores[s] = part
-            run = jnp.maximum(part, jnp.where(r == previous(s), run, FLOOR))
-            runs[s] = run
+            request = [req_ref[s], req_ref[s + 1]]
+            safe = [jnp.maximum(r, 0) for r in request]
+            both = jnp.concatenate([gath1[r].reshape(32, HD) for r in safe], axis=0)
+            product = dot(both, turned_keys[i * (UNROLL // 2) + u // 2])
+            for v in range(2):
+                r = request[v]
+                live = jnp.where(r >= 0, ctx_ref[safe[v]] - start_ref[s + v], 0)
+                part = product[32 * v : 32 * v + 32, BLOCK * v : BLOCK * v + BLOCK]
+                part = jnp.where(token < live, part, FLOOR)
+                scores[s + v] = part
+                run = jnp.maximum(part, jnp.where(r == previous(s + v), run, FLOOR))
+                runs[s + v] = run
         return run
 
     floor_tile = jnp.full((32, BLOCK), FLOOR, F32)
@@ -375,15 +389,20 @@
 
     def value_step(i, carry):
         sum_run, out_run = carry
-        for u in range(UNROLL):
+        for u in range(0, UNROLL, 2):
             s = i * UNROLL + u
-            r = req_ref[s]
-            keep = jnp.where(r == previous(s), 1.0, 0.0).astype(F32)
-            weight = jnp.exp2((scores[s] - tops[jnp.maximum(r, 0)]) * EXP_SCALE)
-            sum_run = sum_run * keep + weight
-            out_run = out_run * keep + dot(weight.astype(BF16), values[s])
-            sums[s] = sum_run
-            outs[s] = out_run
+            weight = [
+                jnp.exp2((scores[s + v] - tops[jnp.maximum(req_ref[s + v], 0)]) * EXP_SCALE) for v in range(2)
+            ]
+            product = dot(
+                jnp.concatenate(weight, axis=0).astype(BF16), jnp.concatenate([values[s], values[s + 1]], axis=1)
+            )
+            for v in range(2):
+                keep = jnp.where(req_ref[s + v] == previous(s + v), 1.0, 0.0).astype(F32)
+                sum_run = sum_run * keep + weight[v]
+                out_run = out_run * keep + product[32 * v : 32 * v + 32, HD * v : HD * v + HD]
+                sums[s + v] = sum_run
+                outs[s + v] = out_run
         return sum_run, out_run
 
     zero_tile = jnp.zeros((32, BLOCK), F32)
@@ -619,6 +638,7 @@
         pltpu.VMEM((nk - 1, 16, 384), BF16),
         pltpu.VMEM((nk, 2, 16, HD), BF16),
         pltpu.VMEM((nm, 2, 16, HD), BF16),
+        pltpu.VMEM((slots // 2, HD, 2 * BLOCK), BF16),
         pltpu.VMEM((slots, 32, BLOCK), F32),
         pltpu.VMEM((slots, 32, BLOCK), F32),
         pltpu.VMEM((nk, 32, BLOCK), F32),

time: 74.3 us -> 70.6 us (0.950)
  Pallas kernels: 73.4 us -> 69.7 us
    pallas_call x1, Pallas kernels: 71.9 us -> 68.2 us  [body(): pl.pallas_call(functools.partial(kernel, nk, nh, db * nk), out_shape=(jax...]
where the time goes in v4:
time: 70.6 us; the launch traced here: 70.4 us
  Pallas kernels  69.7 us (99%)
    pallas_call x1, Pallas kernels, body(): pl.pallas_call(functools.partial(kernel, nk, nh, db * nk), out_shape=(jax...  68.2 us
    pallas_call x1, Pallas kernels, body(): pl.pallas_call(hand_on, out_shape=tuple((jax.ShapeDtypeStruct(r.shape, r....  1.5 us

profile of v4, /device:TPU:1, one launch (start us, length us, event | category | flops | bytes accessed | tf_op | source)
XLA Modules:
  0.0 70.4 jit_solution(8895994591553034028)
XLA Ops:
  0.6 68.2 %shard_map.175 = (bf16[64,512]{1,0:T(8,128)(2,1)}, bf16[64,128]{1,0:T(8,128)(2,1)}, bf16[64,128]{1,0:T(8,128)(2,1)}) custom-call(bf16[64,512]{1,0:T(8,128)(2,1)} %hid_ref.1, bf16[512]{0:T(512)(128)(2,1)} %gain_ref.1, bf16[512]{0:T(512)(128)(2,1)} %post_ref.1, f32[1,128]{1,0:T(1,128)} %constant.2.clone.freq_ref, bf16[512,1024]{1,0:T(8,128)(2,1)} %wq_hbm.1, ...), custom_call_target="tpu_custom_call" | custom-call | flops 1191182336 | bytes 23855104 | tf_op jit(solution)/shard_map/pallas_call | solution.py:674
  68.9 1.5 %shard_map.176 = (bf16[64,512]{1,0:T(8,128)(2,1)}, bf16[64,128]{1,0:T(8,128)(2,1)}, bf16[64,128]{1,0:T(8,128)(2,1)}) custom-call(bf16[64,512]{1,0:T(8,128)(2,1)} %get-tuple-element.6.a_ref, bf16[64,128]{1,0:T(8,128)(2,1)} %get-tuple-element.7.b_ref, bf16[64,128]{1,0:T(8,128)(2,1)} %get-tuple-element.8.c_ref), custom_call_target="tpu_custom_call" | custom-call | tf_op jit(solution)/shard_map/pallas_call | solution.py:710

commit v5 on v4

--- a/solution.py
+++ b/solution.py
@@ -56,10 +56,10 @@
     nk,
     nh,
     width,
-    hid_ref,
-    gain_ref,
-    post_ref,
-    freq_ref,
+    hid_hbm,
+    gain_hbm,
+    post_hbm,
+    freq_hbm,
     wq_hbm,
     wk_hbm,
     wv_hbm,
@@ -69,12 +69,19 @@
     wd_hbm,
     keys_hbm,
     values_hbm,
+    ctx_hbm,
+    req_hbm,
+    start_hbm,
+    next_ref,
+    dkey_ref,
+    dval_ref,
+    hid_ref,
+    gain_ref,
+    post_ref,
+    freq_ref,
     ctx_ref,
     req_ref,
     start_ref,
-    next_ref,
-    dkey_ref,
-    dval_ref,
     wq,
     wk,
     wv,
@@ -144,9 +151,38 @@
 
     sent = []
 
+    offsets = [(dy, dx) for dy in range(side) for dx in range(side) if dy or dx]
+    offsets.sort(key=lambda o: -sum(min(d, side - d) for d in o))
+    targets = [
+        lax.rem(me_y + dy, side) * side + lax.rem(me_x + dx, side) for dy, dx in offsets
+    ]
+    sources = [
+        lax.rem(me_y + side - dy, side) * side + lax.rem(me_x + side - dx, side) for dy, dx in offsets
+    ]
+    near_first = list(reversed(range(nk - 1)))
+    barrier = pltpu.get_barrier_semaphore()
+    for to in targets:
+        pl.semaphore_signal(barrier, inc=1, device_id=(to, me_h), device_id_type=MESH)
+    for to in [twin] + [along_z(k) for k in range(1, nz)]:
+        pl.semaphore_signal(barrier, inc=1, device_id=(me_k, to), device_id_type=MESH)
+
     first_copies = [
         pltpu.make_async_copy(src, dst, local_sem.at[i])
         for i, (src, dst) in enumerate([(wq_hbm, wq), (wk_hbm, wk), (wv_hbm, wv)])
+    ]
+    small_copies = [
+        pltpu.make_async_copy(src, dst, local_sem.at[9 + i])
+        for i, (src, dst) in enumerate(
+            [
+                (hid_hbm, hid_ref),
+                (gain_hbm, gain_ref),
+                (post_hbm, post_ref),
+                (freq_hbm, freq_ref),
+                (ctx_hbm, ctx_ref),
+                (req_hbm, req_ref),
+                (start_hbm, start_ref),
+            ]
+        )
     ]
     later_copies = [
         pltpu.make_async_copy(src, dst, local_sem.at[3 + i])
@@ -157,25 +193,9 @@
     def arrive(i):
         later_copies[i].wait()
 
-    for c in first_copies:
+    for c in small_copies + first_copies:
         c.start()
 
-    barrier = pltpu.get_barrier_semaphore()
-
-    offsets = [(dy, dx) for dy in range(side) for dx in range(side) if dy or dx]
-    offsets.sort(key=lambda o: -sum(min(d, side - d) for d in o))
-    targets = [
-        lax.rem(me_y + dy, side) * side + lax.rem(me_x + dx, side) for dy, dx in offsets
-    ]
-    sources = [
-        lax.rem(me_y + side - dy, side) * side + lax.rem(me_x + side - dx, side) for dy, dx in offsets
-    ]
-    near_first = list(reversed(range(nk - 1)))
-
-    for to in targets:
-        pl.semaphore_signal(barrier, inc=1, device_id=(to, me_h), device_id_type=MESH)
-    for to in [twin] + [along_z(k) for k in range(1, nz)]:
-        pl.semaphore_signal(barrier, inc=1, device_id=(me_k, to), device_id_type=MESH)
 
     def kvp_copy(phase, i, src, dst):
         return pltpu.make_async_remote_copy(
@@ -244,16 +264,12 @@
     def halves(x):
         return x[:, :half], x[:, half:]
 
-    def own_half(x):
-        left, right = halves(x)
-        return jnp.where(core == 0, left, right), jnp.where(core == 0, right, left)
-
-    def head_sum(base, part, swap_ref, along_ref):
-        own, other = own_half(part)
-        swap_ref[0] = other.astype(BF16)
+    def head_sum(base, part_of, swap_ref, along_ref):
+        swap_ref[0] = part_of(1 - core).astype(BF16)
         swapped = head_copy(base, twin, swap_ref.at[0], swap_ref.at[1])
         swapped.start()
         sent.append(swapped)
+        own = part_of(core)
         swapped.wait_recv()
         along_ref[0] = (own + swap_ref[1].astype(F32)).astype(BF16)
         copies = [head_copy(base + k, along_z(k), along_ref.at[0], along_ref.at[k]) for k in range(1, nz)]
@@ -280,6 +296,8 @@
     def folded(x):
         return jnp.concatenate([x[:, : x.shape[1] // 2], x[:, x.shape[1] // 2 :]], axis=0)
 
+    for c in small_copies:
+        c.wait()
     hidden = hid_ref[...].astype(F32)
     hidden_halves[0], hidden_halves[1] = halves(hidden)
     scaled = (hidden * gain_ref[...].astype(F32).reshape(1, db)).astype(BF16)
@@ -483,14 +501,17 @@
     arrive(2)
     kvp_gather_wait(3, lambda source: gath2.at[source // 2, source % 2])
 
-    attn_part = jnp.zeros((rows, db), F32)
-    for c in range(2):
-        for g in range(2):
-            piece = jnp.concatenate(
-                [gath2[m, c].astype(F32)[8 * g : 8 * g + 8] for m in range(nm)], axis=0
-            ).astype(BF16)
-            attn_part += dot(piece, wo[512 * c + 256 * g : 512 * c + 256 * g + 256, :])
-    attn = head_sum(0, attn_part, core3, along3)
+    heads = [
+        jnp.concatenate([gath2[m, c].astype(F32)[8 * g : 8 * g + 8] for m in range(nm)], axis=0).astype(BF16)
+        for c in range(2)
+        for g in range(2)
+    ]
+
+    def attn_half(which):
+        columns = pl.ds(pl.multiple_of(which * half, half), half)
+        return sum(dot(heads[n], wo[256 * n : 256 * n + 256, columns]) for n in range(4))
+
+    attn = head_sum(0, attn_half, core3, along3)
     resid[core] = (hidden_halves[core] + attn).astype(BF16)
     share_half(nz, resid)
     residual = jnp.concatenate([resid[0].astype(F32), resid[1].astype(F32)], axis=1)
@@ -524,7 +545,6 @@
             send_sq[:, 0] = square_out
             send_sq[:, 1] = square_out
             kvp_scatter(4, send_sq, recv_sq)
-    finish()
     for p, part in direct:
         for i, to in enumerate(targets):
             src = send4.at[to // side, (to % side) // 2, to % 2, :, part]
@@ -560,7 +580,8 @@
     total = kvp_reduce(4, send_sq[me_m, me_c], recv_sq)
     inverse = lax.rsqrt(jnp.sum(total[:8], axis=1, keepdims=True) / width + EPSILON)
     base = 5 + len(pieces)
-    for p, (at, size, axis) in enumerate(pieces):
+    order = [2, 0, 1]
+    for p, (at, size, axis) in [(p, pieces[p]) for p in order]:
         part = pl.ds(at, size)
         if axis is None:
             own = send4[me_y, me_x // 2, me_c, :, part]
@@ -580,7 +601,7 @@
     finish()
     arrive(5)
     down_part = jnp.zeros((rows, db), F32)
-    for p, (at, size, _) in enumerate(pieces):
+    for p, (at, size, _) in [(p, pieces[p]) for p in order]:
         part = pl.ds(at // 2, size // 2)
         kvp_gather_wait(base + p, lambda source, part=part: gath4.at[source // 2, source % 2, :, part])
         for c in range(2):
@@ -590,7 +611,7 @@
                 axis=1,
             ).astype(BF16)
             down_part += dot(piece, wd[c * fh + at : c * fh + at + size, :])
-    down = head_sum(nz + 1, down_part, core5, along5)
+    down = head_sum(nz + 1, lambda which: jnp.where(which == 0, *halves(down_part)), core5, along5)
     final[core] = (resid[core].astype(F32) + down).astype(BF16)
     share_half(2 * nz + 1, final)
     next_ref[:, :half] = final[0]
@@ -627,8 +648,16 @@
     frequency = jnp.asarray(np.concatenate([frequency, frequency])[None, :])
     vmem = pl.BlockSpec(memory_space=pltpu.VMEM)
     hbm = pl.BlockSpec(memory_space=pl.ANY)
-    smem = pl.BlockSpec(memory_space=pltpu.SMEM)
     scratch = [
+        pltpu.VMEM(hidden_in.shape, BF16),
+        pltpu.VMEM(norm_gain.shape, BF16),
+        pltpu.VMEM(post_gain.shape, BF16),
+        pltpu.VMEM(frequency.shape, F32),
+        pltpu.SMEM(context_len.shape, jnp.int32),
+        pltpu.SMEM(slot_request.shape, jnp.int32),
+        pltpu.SMEM(slot_start.shape, jnp.int32),
+    ]
+    scratch += [
         pltpu.VMEM(w.shape, BF16)
         for w in (w_query, w_key, w_value, w_out, w_gate, w_up, w_down, cache_keys, cache_values)
     ]
@@ -662,7 +691,7 @@
         pltpu.VMEM((2, rows, half), BF16),
         pltpu.VMEM((nz, rows, half), BF16),
         pltpu.VMEM((2, rows, half), BF16),
-        pltpu.SemaphoreType.DMA((9,)),
+        pltpu.SemaphoreType.DMA((16,)),
         pltpu.SemaphoreType.DMA((6 + 2 * count, nk)),
         pltpu.SemaphoreType.DMA((6 + 2 * count, nk)),
         pltpu.SemaphoreType.DMA((2 * nz + 2,)),
@@ -678,7 +707,7 @@
             jax.ShapeDtypeStruct((rows, HD), BF16),
             jax.ShapeDtypeStruct((rows, HD), BF16),
         ),
-        in_specs=[vmem] * 4 + [hbm] * 9 + [smem] * 3,
+        in_specs=[hbm] * 16,
         out_specs=(vmem, vmem, vmem),
         scratch_shapes=scratch,
         compiler_params=pltpu.CompilerParams(

time: 70.6 us -> 69.7 us (0.987)
  Pallas kernels: 69.7 us -> 68.9 us
    pallas_call x1, Pallas kernels: 68.2 us -> 67.4 us  [body(): pl.pallas_call(functools.partial(kernel, nk, nh, db * nk), out_shape=(jax...]
where the time goes in v5:
time: 69.7 us; the launch traced here: 69.5 us
  Pallas kernels  68.9 us (99%)
    pallas_call x1, Pallas kernels, body(): pl.pallas_call(functools.partial(kernel, nk, nh, db * nk), out_shape=(jax...  67.4 us
    pallas_call x1, Pallas kernels, body(): pl.pallas_call(hand_on, out_shape=tuple((jax.ShapeDtypeStruct(r.shape, r....  1.5 us

profile of v5, /device:TPU:1, one launch (start us, length us, event | category | flops | bytes accessed | tf_op | source)
XLA Modules:
  0.0 69.5 jit_solution(10889721429490228306)
XLA Ops:
  0.6 67.4 %shard_map.175 = (bf16[64,512]{1,0:T(8,128)(2,1)}, bf16[64,128]{1,0:T(8,128)(2,1)}, bf16[64,128]{1,0:T(8,128)(2,1)}) custom-call(bf16[64,512]{1,0:T(8,128)(2,1)} %hid_hbm.1, bf16[512]{0:T(512)(128)(2,1)} %gain_hbm.1, bf16[512]{0:T(512)(128)(2,1)} %post_hbm.1, f32[1,128]{1,0:T(1,128)} %constant.2.clone.freq_hbm, bf16[512,1024]{1,0:T(8,128)(2,1)} %wq_hbm.1, ...), custom_call_target="tpu_custom_call" | custom-call | flops 1191182336 | bytes 23855104 | tf_op jit(solution)/shard_map/pallas_call | solution.py:703
  68.1 1.5 %shard_map.176 = (bf16[64,512]{1,0:T(8,128)(2,1)}, bf16[64,128]{1,0:T(8,128)(2,1)}, bf16[64,128]{1,0:T(8,128)(2,1)}) custom-call(bf16[64,512]{1,0:T(8,128)(2,1)} %get-tuple-element.6.a_ref, bf16[64,128]{1,0:T(8,128)(2,1)} %get-tuple-element.7.b_ref, bf16[64,128]{1,0:T(8,128)(2,1)} %get-tuple-element.8.c_ref), custom_call_target="tpu_custom_call" | custom-call | tf_op jit(solution)/shard_map/pallas_call | solution.py:739

commit v6 on v5

--- a/solution.py
+++ b/solution.py
@@ -17,7 +17,7 @@
 FLOOR = -1e30
 LOG2E = math.log2(math.e)
 EXP_SCALE = LOG2E / math.sqrt(HD)
-UNROLL = 80
+UNROLL = 160
 MESH = pl.DeviceIdType.MESH
 F32 = jnp.float32
 BF16 = jnp.bfloat16

time: 69.7 us -> 69.5 us (level)
  no operation moved by 1% of the time
where the time goes in v6:
time: 69.5 us; the launch traced here: 69.1 us
  Pallas kernels  68.5 us (99%)
    pallas_call x1, Pallas kernels, body(): pl.pallas_call(functools.partial(kernel, nk, nh, db * nk), out_shape=(jax...  67 us
    pallas_call x1, Pallas kernels, body(): pl.pallas_call(hand_on, out_shape=tuple((jax.ShapeDtypeStruct(r.shape, r....  1.5 us

profile of v6, /device:TPU:1, one launch (start us, length us, event | category | flops | bytes accessed | tf_op | source)
XLA Modules:
  0.0 69.1 jit_solution(4008252510836318569)
XLA Ops:
  0.6 67.0 %shard_map.175 = (bf16[64,512]{1,0:T(8,128)(2,1)}, bf16[64,128]{1,0:T(8,128)(2,1)}, bf16[64,128]{1,0:T(8,128)(2,1)}) custom-call(bf16[64,512]{1,0:T(8,128)(2,1)} %hid_hbm.1, bf16[512]{0:T(512)(128)(2,1)} %gain_hbm.1, bf16[512]{0:T(512)(128)(2,1)} %post_hbm.1, f32[1,128]{1,0:T(1,128)} %constant.2.clone.freq_hbm, bf16[512,1024]{1,0:T(8,128)(2,1)} %wq_hbm.1, ...), custom_call_target="tpu_custom_call" | custom-call | flops 1191182336 | bytes 23855104 | tf_op jit(solution)/shard_map/pallas_call | solution.py:703
  67.6 1.5 %shard_map.176 = (bf16[64,512]{1,0:T(8,128)(2,1)}, bf16[64,128]{1,0:T(8,128)(2,1)}, bf16[64,128]{1,0:T(8,128)(2,1)}) custom-call(bf16[64,512]{1,0:T(8,128)(2,1)} %get-tuple-element.6.a_ref, bf16[64,128]{1,0:T(8,128)(2,1)} %get-tuple-element.7.b_ref, bf16[64,128]{1,0:T(8,128)(2,1)} %get-tuple-element.8.c_ref), custom_call_target="tpu_custom_call" | custom-call | tf_op jit(solution)/shard_map/pallas_call | solution.py:739
